TPU v7x, 256 devices: a whole 4x4x8 slice. The times are simulated.
256 devices in a mesh: seg: 16 (over z, core), term: 16 (over x, y).
Axes of the slice: x: 4, y: 4, z: 8, core: 2. Of those that a mesh axis runs over, the one named last changes fastest.
Arguments:
- wave_in: float32 [16, 16, 128, 128], P('seg')
- env_left: float32 [16, 64, 16, 128, 128], P('seg', 'term'), may hold values from -0.0625 to 0.0625
- env_right: float32 [16, 64, 16, 128, 128], P('seg', 'term'), may hold values from -0.5 to 0.5
- sector_charge: int32 [16, 2], replicated, may hold values from 0 to 3, as said below
- term_charge: int32 [64, 2], P('term'), may hold values from -1 to 1, as said below
- term_live: int32 [64], P('term'), may hold values from 0 to 1, as said below
- transfer: float32 [16, 16, 128, 128], P('seg'), may hold values from -0.15625 to 0.15625
Outputs:
- wave_out: float32 [16, 16, 128, 128], P('seg', 'term')
- new_env: float32 [16, 16, 128, 128], P('seg', 'term')
Inputs may be any that keep to these rules, and one draw needn't show every extreme that they name: `sector_charge`: each of the 16 pairs (up, down) with both numbers in 0 .. 3 labels exactly one sector. `term_charge`: each term changes at most one of the two particle numbers, by one. `term_live`: in every draw some aligned group of 4 terms is all live.
All inputs are finite; a program needn't handle non-finite values.
Results may differ from a plain program's by a relative error of at most 0.0003.
Values sent between devices are 32-bit elements; how exact they have to be, the bound alone decides.
A program may use at most 128 MiB of HBM per device.

v0:
```python
import jax
import jax.numpy as jnp
from jax import lax
from jax.sharding import PartitionSpec as P

ITERS = 3


mean_eps = 1e-06
step_size = 0.5
HIGH = lax.Precision.HIGHEST


def prefix_2(x, axis, combine, identity):
    devices, mine = (lax.axis_size(axis), lax.axis_index(axis))
    everything = jax.tree.map(lambda part: lax.all_gather(part, axis), x)
    start = jax.tree.map(
        lambda part, zero: jnp.broadcast_to(jnp.asarray(zero, part.dtype), part.shape), x, identity
    )

    def hop(k, before):
        reached = k < mine
        new = combine(before, jax.tree.map(lambda part: part[k], everything))
        return jax.tree.map(lambda a, b: jnp.where(reached, a, b), new, before)

    return lax.fori_loop(0, devices, hop, start)


def source_tables(sector_charge, term_charge):
    target = sector_charge[None, :, :] - term_charge[:, None, :]
    match = jnp.all(target[:, :, None, :] == sector_charge[None, None, :, :], axis=3)
    return match.astype(jnp.float32)


def term_image(wave, table, left, right):
    moved = jnp.einsum("st,tbc->sbc", table, wave, precision=HIGH)
    inner = jnp.einsum("sab,sbc->sac", left, moved, precision=HIGH)
    return jnp.einsum("sac,sdc->sad", inner, right, precision=HIGH)


def normalize(wave):
    return wave * lax.rsqrt(jnp.mean(wave * wave) + mean_eps)


def partial_image(wave, tables, term_live, left, right):
    flags = term_live.astype(jnp.float32)

    def add_slot(index, total):
        return total + flags[index] * term_image(wave, tables[index], left[index], right[index])

    return lax.fori_loop(0, tables.shape[0], add_slot, jnp.zeros_like(wave))


def link(earlier, later):
    first_map, first_sum = earlier
    second_map, second_sum = later
    joined = jnp.einsum("sab,sbc->sac", first_map, second_map, precision=HIGH)
    inner = jnp.einsum("sba,sbc->sac", second_map, first_sum, precision=HIGH)
    moved = jnp.einsum("sac,scd->sad", inner, second_map, precision=HIGH)
    return (joined, moved + second_sum)


def finish(step_map, carried):
    inner = jnp.einsum("sba,sbc->sac", step_map, carried, precision=HIGH)
    return jnp.einsum("sac,scd->sad", inner, step_map, precision=HIGH)


def shards(wave_in, env_left, env_right, sector_charge, term_charge, term_live, transfer):
    tables = source_tables(sector_charge, term_charge)
    left = env_left[0]
    right = env_right[0]
    sectors = wave_in.shape[1]
    block = wave_in.shape[2]
    per_dev = sectors // lax.axis_size("term")
    start = lax.axis_index("term") * per_dev
    eye_block = jnp.eye(block, dtype=jnp.float32)
    wave = normalize(wave_in[0])
    image = jnp.zeros_like(wave)
    for step in range(ITERS):
        partial_value = partial_image(wave, tables, term_live, left, right)
        image = lax.psum(partial_value, "term")
        theta = jnp.mean(wave * image)
        wave = normalize(wave - step_size * (image - theta * wave))
    energy = jnp.einsum("sab,sac->sbc", wave, image, precision=HIGH) / block
    step_map = eye_block[None] + transfer[0]
    identity = (jnp.broadcast_to(eye_block, step_map.shape), jnp.zeros_like(energy))
    prefix = prefix_2((step_map, energy), "seg", link, identity)
    carried = finish(step_map, prefix[1])
    wave_share = lax.dynamic_slice_in_dim(wave, start, per_dev, 0)
    env_share = lax.dynamic_slice_in_dim(carried, start, per_dev, 0)
    return (wave_share[None], env_share[None])


def solution(mesh):
    in_specs = (
        P("seg", None, None, None),
        P("seg", "term", None, None, None),
        P("seg", "term", None, None, None),
        P(),
        P("term", None),
        P("term"),
        P("seg", None, None, None),
    )
    out_specs = (P("seg", "term", None, None), P("seg", "term", None, None))
    return jax.shard_map(shards, mesh=mesh, in_specs=in_specs, out_specs=out_specs, check_vma=False)
```

profile of v0, /device:TPU:1, one launch (start us, length us, event | category | flops | bytes accessed | tf_op | source)
XLA Modules:
  0.0 643.0 jit_solution(18386446251573633169)
XLA Ops:
  15.8 34.2 %while.56 = (s32[]{:T(128)}, f32[16,128,128]{2,1,0:T(8,128)S(1)}, f32[4]{0:T(128)S(1)}, f32[4,16,128,128]{3,2,1,0:T(8,128)}, f32[4,16,16]{2,1,0:T(8,128)S(1)}, /...) while((s32[]{:T(128)}, f32[16,128,128]{2,1,0:T(8,128)S(1)}, ...), condition=%wide.region_3.0_spmd.clone, body=%wide.region_2.0_spmd.clone.sunk | while | flops 856424448 | bytes 9446023 | solution.py:51
  20.0 4.3 fusion.108
  25.9 2.6 fusion.107
  28.6 4.3 fusion.108
  34.5 2.6 fusion.107
  37.1 4.3 fusion.108
  43.0 2.6 fusion.107
  45.7 4.3 fusion.108
  51.1 99.6 %all-reduce.4.cloned.1.call-done = f32[16,128,128]{2,1,0:T(8,128)} async-done(((f32[16,128,128]{2,1,0:T(8,128)}), f32[16,128,128]{2,1,0:T(8,128)}) %all-reduce.4.cloned.1.call-update) | async-done | bytes 1048592 | tf_op jit(solution)/shard_map/psum | solution.py:81
  158.1 34.2 %while.57 = (s32[]{:T(128)}, f32[16,128,128]{2,1,0:T(8,128)S(1)}, f32[4]{0:T(128)S(1)}, f32[4,16,128,128]{3,2,1,0:T(8,128)}, f32[4,16,16]{2,1,0:T(8,128)S(1)}, /...) while((s32[]{:T(128)}, f32[16,128,128]{2,1,0:T(8,128)S(1)}, ...), condition=%wide.region_8.0_spmd.clone, body=%wide.region_7.0_spmd.clone.sunk | while | flops 856424448 | bytes 9446023 | solution.py:51
  159.8 2.6 fusion.116
  162.4 4.3 fusion.117
  168.3 2.6 fusion.116
  171.0 4.3 fusion.117
  176.9 2.6 fusion.116
  179.5 4.3 fusion.117
  185.4 2.6 fusion.116
  188.0 4.3 fusion.117
  193.6 96.4 %all-reduce.6.cloned.1.call-done = f32[16,128,128]{2,1,0:T(8,128)} async-done(((f32[16,128,128]{2,1,0:T(8,128)}), f32[16,128,128]{2,1,0:T(8,128)}) %all-reduce.6.cloned.1.call-update) | async-done | bytes 1048592 | tf_op jit(solution)/shard_map/psum | solution.py:81
  297.6 34.2 %while.58 = (s32[]{:T(128)}, f32[16,128,128]{2,1,0:T(8,128)S(1)}, f32[4]{0:T(128)S(1)}, f32[4,16,128,128]{3,2,1,0:T(8,128)}, f32[4,16,16]{2,1,0:T(8,128)S(1)}, /...) while((s32[]{:T(128)}, f32[16,128,128]{2,1,0:T(8,128)S(1)}, ...), condition=%wide.region_13.0_spmd.clone, body=%wide.region_12.0_spmd.clone.sunk | while | flops 856424448 | bytes 9446023 | solution.py:51
  299.2 2.6 fusion.125
  301.8 4.3 fusion.126
  307.7 2.6 fusion.125
  310.4 4.3 fusion.126
  316.3 2.6 fusion.125
  318.9 4.3 fusion.126
  324.8 2.6 fusion.125
  327.4 4.3 fusion.126
  335.2 94.2 %all-reduce.8.cloned.1.call-done = f32[16,128,128]{2,1,0:T(8,128)} async-done(((f32[16,128,128]{2,1,0:T(8,128)}), f32[16,128,128]{2,1,0:T(8,128)}) %all-reduce.8.cloned.1.call-update) | async-done | bytes 1048592 | tf_op jit(solution)/shard_map/psum | solution.py:81
  435.3 2.9 convolution_multiply_fusion.3
  438.9 95.9 %all-gather.6.cloned.1.call-done = f32[256,128,128]{2,1,0:T(8,128)} async-done(((f32[16,128,128]{2,1,0:T(8,128)}), f32[256,128,128]{2,1,0:T(8,128)}) %all-gather.6.cloned.1.call-update) | async-done | bytes 16777232 | tf_op jit(solution)/shard_map/all_gather | solution.py:16
  534.7 97.5 %while.59 = (s32[]{:T(128)}, f32[16,128,128]{2,1,0:T(8,128)S(1)}, s32[]{:T(128)}, f32[16,16,128,128]{3,2,1,0:T(8,128)}, f32[16,16,128,128]{3,2,1,0:T(8,128)}, /*index=5*/s32[]{:T(128)}, s32[]{:T(128)}) while((s32[]{:T(128)}, f32[16,128,128]{2,1,0:T(8,128)S(1)}, s32[]{:T(128)}, f32[16,16,128,128]{3,2,1,0:T(8,128)}, ...), condition=%wide.region_18.19_spmd.clone, body=%wide.region_17.18_spmd.clone.sunk | while | flops 806354944 | bytes 8390764 | solution.py:26
  534.7 3.1 fusion.131
  537.9 3.0 fusion.132
  540.9 3.1 fusion.131
  543.9 3.0 fusion.132
  547.0 3.1 fusion.131
  550.0 3.0 fusion.132
  553.0 3.1 fusion.131
  556.1 3.0 fusion.132
  559.1 3.1 fusion.131
  562.2 3.0 fusion.132
  565.2 3.1 fusion.131
  568.3 3.0 fusion.132
  571.3 3.1 fusion.131
  574.3 3.0 fusion.132
  577.4 3.1 fusion.131
  580.4 3.0 fusion.132
  583.4 3.1 fusion.131
  586.5 3.1 fusion.132
  589.6 3.1 fusion.131
  592.7 3.0 fusion.132
  595.7 3.1 fusion.131
  598.8 3.0 fusion.132
  601.8 3.1 fusion.131
  604.8 3.0 fusion.132
  607.9 3.1 fusion.131
  610.9 3.0 fusion.132
  614.0 3.1 fusion.131
  617.0 3.0 fusion.132
  620.1 3.1 fusion.131
  623.1 3.0 fusion.132
  626.1 3.1 fusion.131
  629.2 3.0 fusion.132
  (85 shorter events, 55.7 us)
Async XLA Ops:
  8.0 142.7 %all-reduce.4.cloned.1.call-start = ((), (), s32[]{:S(2)}) async-start(), calls=%async_computation | async-start | bytes 2097152 | tf_op jit(solution)/shard_map/psum | solution.py:81
  15.7 134.9 %copy-start.3 = (f32[1,16,128,128]{3,2,1,0:T(8,128)S(1)}, f32[1,16,128,128]{3,2,1,0:T(8,128)}, u32[]{:S(2)}) copy-start(f32[1,16,128,128]{3,2,1,0:T(8,128)} %param.15) | copy-start | bytes 3145732
  50.0 1.0 copy-start.2
  51.0 238.9 %all-reduce.6.cloned.1.call-start = ((), (), s32[]{:S(2)}) async-start(), calls=%async_computation.1 | async-start | bytes 2097152 | tf_op jit(solution)/shard_map/psum | solution.py:81
  150.6 5.6 copy-start.9
  156.5 1.0 copy-start.4
  158.1 131.8 %copy-start.5 = (f32[16,128,128]{2,1,0:T(8,128)S(1)}, f32[16,128,128]{2,1,0:T(8,128)}, u32[]{:S(2)}) copy-start(f32[16,128,128]{2,1,0:T(8,128)} %copy-done.4) | copy-start | bytes 3145732
  192.3 1.0 copy-start
  192.4 103.2 %copy-start.6 = (f32[16,128,128]{2,1,0:T(8,128)S(1)}, f32[16,128,128]{2,1,0:T(8,128)}, u32[]{:S(2)}) copy-start(f32[16,128,128]{2,1,0:T(8,128)} %copy-done.4) | copy-start | bytes 3145732
  193.4 236.1 %all-reduce.8.cloned.1.call-start = ((), (), s32[]{:S(2)}) async-start(), calls=%async_computation.2 | async-start | bytes 2097152 | tf_op jit(solution)/shard_map/psum | solution.py:81
  331.7 1.0 copy-start.1
  332.8 106.0 %all-gather.4.cloned.1.call-start = ((), (), s32[]{:S(2)}) async-start(), calls=%async_computation.3 | async-start | bytes 17825792 | tf_op jit(solution)/shard_map/all_gather | solution.py:16
  335.2 199.5 %all-gather.6.cloned.1.call-start = ((), (), s32[]{:S(2)}) async-start(), calls=%async_computation.4 | async-start | bytes 17825792 | tf_op jit(solution)/shard_map/all_gather | solution.py:16
  429.5 5.6 copy-start.7
  534.7 97.5 %copy-start.8 = (f32[1,16,128,128]{3,2,1,0:T(8,128)S(1)}, f32[1,16,128,128]{3,2,1,0:T(8,128)}, u32[]{:S(2)}) copy-start(f32[1,16,128,128]{3,2,1,0:T(8,128)} %param.21) | copy-start | bytes 3145732
Sparse Core Ops, SparseCore 0:
  51.1 99.4 all-reduce.3
  193.5 96.4 all-reduce.5
  332.9 96.4 all-reduce.7
Sparse Core Ops, SparseCore 1:
  335.3 96.5 all-gather.3
  438.3 96.4 all-gather.5
where the time goes:
time: 646 us; the launch traced here: 643 us
  waiting for transfers between devices  386 us (60%)
  matrix products  198 us (31%)
  other arithmetic  22.5 us (3%)
  between operations  20.2 us (3%)
  local copies, waits for them, and re-layouts  14.9 us (2%)
    psum x3, waiting for transfers between devices, shards(): image = lax.psum(partial_value, 'term')  290 us
    all_gather x2, waiting for transfers between devices, prefix_2(): everything = jax.tree.map(lambda part: lax.all_gather(part, axis), x)  95.9 us
    dot_general x12, matrix products, term_image(): return jnp.einsum('sac,sdc->sad', inner, right, precision=HIGH)  51.4 us
    dot_general x16, matrix products, link(): inner = jnp.einsum('sba,sbc->sac', second_map, first_sum, precision=HIGH)  49 us
    dot_general x16, matrix products, link(): moved = jnp.einsum('sac,scd->sad', inner, second_map, precision=HIGH)  47.9 us
    dot_general x12, matrix products, term_image(): inner = jnp.einsum('sab,sbc->sac', left, moved, precision=HIGH)  31.6 us
  transfers between devices with their start and end apart: 5, of which 4 were waited for; matrix products, arithmetic and copies ran while one was open for 2% of the time, Pallas kernels for 0%

commit v1 on v0

v1 whole, which is shorter than its diff:
```python
import functools

import jax
import jax.numpy as jnp
from jax import lax
from jax.experimental import pallas as pl
from jax.experimental.pallas import tpu as pltpu
from jax.sharding import PartitionSpec as P

ITERS = 3
SIDE = 4
CHARGES = 4
BK = 128
HALF = 64
NS = 16
SLOTS = 4
NSEG = 16
ROUNDS = 4
ENTRIES = float(NS * BK * BK)
mean_eps = 1e-06
step_size = 0.5

F32 = jnp.float32
BF16 = jnp.bfloat16
MESH = pl.DeviceIdType.MESH


def split(x):
    high = x.astype(BF16)
    low = (x - high.astype(F32)).astype(BF16)
    return high, low


def beside(x):
    return jnp.concatenate(split(x), axis=1)


def doubled(x):
    row = beside(x)
    return jnp.concatenate([row, row], axis=0)


def product(left, right):
    both = jnp.dot(left, right, preferred_element_type=F32)
    return both[:, :BK] + both[:, BK:]


def fold(x):
    return jnp.sum(x.reshape(x.shape[0] // 8, 8, x.shape[1]), axis=0)


def far_first(i):
    return (2 + i + i // 2 + 2 * (i // 3)) % 4


def near_first(i):
    return i + i // 2 - 2 * (i // 3)


def kernel(
    sector_ref, term_ref, live_ref, wave_hbm, left_hbm, right_hbm, transfer_hbm,
    wave_out, env_out,
    code, place, source, target, mask,
    stage_l, stage_r, stage_w, stage_t, lcat, rcat, inner, waves, image_parts,
    r1, p2, r2, small, small_in, qs, q_in, qdup, qt, s_out, s_in, env_acc,
    load_sem, s1_send, s1_recv, s2_send, s2_recv, g1_send, g2_send, g_recv,
    small_send, small_recv, q_send, q_recv, c_send, c_recv,
):
    seg = lax.axis_index("seg")
    own = lax.axis_index("term")
    x, y = own // SIDE, own % SIDE

    def at(dx, dy):
        return (seg, ((x + dx) % SIDE) * SIDE + (y + dy) % SIDE)

    load_w = pltpu.make_async_copy(wave_hbm.at[0], stage_w, load_sem.at[0])
    load_t = pltpu.make_async_copy(transfer_hbm.at[0, own], stage_t, load_sem.at[1])
    load_w.start()
    load_t.start()
    load_l = [pltpu.make_async_copy(left_hbm.at[0, w], stage_l.at[w], load_sem.at[2 + w]) for w in range(SLOTS)]
    load_r = [pltpu.make_async_copy(right_hbm.at[0, w], stage_r.at[w], load_sem.at[6 + w]) for w in range(SLOTS)]
    for load in load_l + load_r:
        load.start()
    barrier = pltpu.get_barrier_semaphore()
    greeted = 0
    for d in range(1, SIDE):
        pl.semaphore_signal(barrier, inc=1, device_id=at(d, 0), device_id_type=MESH)
        pl.semaphore_signal(barrier, inc=1, device_id=at(0, d), device_id_type=MESH)
        greeted += 2
    for d in (1, 2, 4, 8, 12, 14, 15):
        pl.semaphore_signal(barrier, inc=1, device_id=((seg + d) % NSEG, own), device_id_type=MESH)
        greeted += 1

    for s in range(NS):
        code[s] = sector_ref[s, 0] * CHARGES + sector_ref[s, 1]

    def find(c, carry):
        found = jnp.int32(0)
        for s in range(NS):
            found = jnp.where(code[s] == c, jnp.int32(s), found)
        place[c] = found
        return carry

    lax.fori_loop(0, NS, find, 0)

    def look_up(w, carry):
        up_change, down_change = term_ref[w, 0], term_ref[w, 1]
        alive = live_ref[w].astype(F32)

        def one(s, carry):
            def sector_at(up, down):
                inside = (up >= 0) & (up < CHARGES) & (down >= 0) & (down < CHARGES)
                return inside, place[jnp.where(inside, up * CHARGES + down, 0)]

            up, down = sector_ref[s, 0], sector_ref[s, 1]
            inside, found = sector_at(up - up_change, down - down_change)
            source[w * NS + s] = found
            mask[w * NS + s] = jnp.where(inside, alive, jnp.float32(0))
            target[w * NS + s] = sector_at(up + up_change, down + down_change)[1]
            return carry

        return lax.fori_loop(0, NS, one, carry)

    lax.fori_loop(0, SLOTS, look_up, 0)

    load_w.wait()

    def add_square(t, total):
        v = stage_w[t]
        return total + fold(v * v)

    def scale_from(squares):
        return lax.rsqrt(jnp.sum(squares) / ENTRIES + mean_eps)

    squares = lax.fori_loop(0, NS, add_square, jnp.zeros((8, BK), F32))
    scale = scale_from(squares)

    def set_wave(t, carry):
        waves[0, t] = stage_w[t] * scale
        return carry

    lax.fori_loop(0, NS, set_wave, 0)

    for w in range(SLOTS):
        load_l[w].wait()

        def set_left(s, carry):
            lcat[w, s] = beside(stage_l[w, s])
            return carry

        lax.fori_loop(0, NS, set_left, 0)

    load_t.wait()
    rows = lax.broadcasted_iota(jnp.int32, (BK, BK), 0)
    columns = lax.broadcasted_iota(jnp.int32, (BK, BK), 1)
    qs[0] = stage_t[...] + jnp.where(rows == columns, jnp.float32(1), jnp.float32(0))
    pl.semaphore_wait(barrier, greeted)

    def chain_copy(src, dst, send, recv, k):
        return pltpu.make_async_remote_copy(
            src_ref=src.at[k], dst_ref=dst.at[k], send_sem=send.at[k], recv_sem=recv.at[k],
            device_id=((seg + 2**k) % NSEG, own), device_id_type=MESH,
        )

    def send_map(k):
        @pl.when(seg + 2**k < NSEG)
        def _():
            chain_copy(qs, q_in, q_send, q_recv, k).start()

    def join_map(k):
        q = qs[k]
        qdup[k] = doubled(q)
        qt[k] = beside(q.T)
        if k + 1 < ROUNDS:
            @pl.when(seg >= 2**k)
            def _():
                chain_copy(qs, q_in, q_send, q_recv, k).wait_recv()
                qs[k + 1] = product(beside(q_in[k]), qdup[k])

            @pl.when(seg < 2**k)
            def _():
                qs[k + 1] = q

            @pl.when(seg + 2**k < NSEG)
            def _():
                chain_copy(qs, q_in, q_send, q_recv, k).wait_send()

    send_map(0)

    def s1_copy(it, side, d, chunk, src):
        return pltpu.make_async_remote_copy(
            src_ref=src, dst_ref=r1.at[it, side, d - 1, chunk],
            send_sem=s1_send.at[side, d - 1, chunk], recv_sem=s1_recv.at[side, d - 1, chunk],
            device_id=at(0, d) if side == 0 else at(d, 0), device_id_type=MESH,
        )

    def s2_copy(it, side, d):
        return pltpu.make_async_remote_copy(
            src_ref=p2.at[it, side, d], dst_ref=r2.at[it, side, d - 1],
            send_sem=s2_send.at[side, d - 1], recv_sem=s2_recv.at[side, d - 1],
            device_id=at(d, 0) if side == 0 else at(0, d), device_id_type=MESH,
        )

    def half(side):
        return pl.ds(side * HALF, HALF)

    def small_copy(it, side, d):
        return pltpu.make_async_remote_copy(
            src_ref=small.at[it, side], dst_ref=small_in.at[it, side, d - 1],
            send_sem=small_send.at[it, side, d - 1], recv_sem=small_recv.at[it, side, d - 1],
            device_id=at(0, d) if side == 0 else at(d, 0), device_id_type=MESH,
        )

    def small_start(it, side, value):
        small[it, side] = value
        for d in (2, 1, 3):
            small_copy(it, side, d).start()

    def small_sum(it, side):
        total = small[it, side]
        for d in (1, 2, 3):
            small_copy(it, side, d).wait_recv()
            total = total + small_in[it, side, d - 1]
        return total

    def small_end(it):
        for side in (0, 1):
            for d in (1, 2, 3):
                small_copy(it, side, d).wait_send()

    def gather_copy(it, sector, side, send, device):
        block = waves.at[it, sector, half(side)]
        return pltpu.make_async_remote_copy(
            src_ref=block, dst_ref=block, send_sem=send, recv_sem=g_recv.at[sector, side],
            device_id=device, device_id_type=MESH,
        )

    def arrived(it, sector, side):
        gather_copy(it, sector, side, g1_send.at[0, 0], at(1, 0)).wait_recv()

    def sector_of(dx, dy):
        return ((x + dx) % SIDE) * SIDE + (y + dy) % SIDE

    def forward(it, side, i):
        sector = sector_of(i, 0) if side == 0 else sector_of(0, i)
        return [
            gather_copy(it, sector, side, g2_send.at[side, i, d - 1], at(0, d) if side == 0 else at(d, 0))
            for d in (2, 1, 3)
        ]

    def first_hop(it):
        return [
            gather_copy(it, own, side, g1_send.at[side, d - 1], at(d, 0) if side == 0 else at(0, d))
            for d in (2, 1, 3) for side in (0, 1)
        ]

    def left_half(it, t, squares):
        v = waves[it, t]
        left = jnp.concatenate([lcat[w, target[w * NS + t]] for w in range(SLOTS)], axis=0)
        high, low = split(product(left, doubled(v)))
        for w in range(SLOTS):
            part = slice(w * BK, (w + 1) * BK)
            inner[w, t] = jnp.concatenate([high[part], low[part]], axis=0)
        return squares + fold(v * v)

    def right_half(it, s, scale):
        left = jnp.concatenate([inner[w, source[w * NS + s]] for w in range(SLOTS)], axis=1)
        both = lax.dot_general(left, rcat[s], (((1,), (1,)), ((), ())), preferred_element_type=F32)
        return (both[:BK, :BK] + both[:BK, BK:] + both[BK:, :BK] + both[BK:, BK:]) * scale

    scale = jnp.float32(1)
    for it in range(ITERS):
        if it == 0:
            lax.fori_loop(0, NS, functools.partial(left_half, 0), jnp.zeros((8, BK), F32))
            for w in range(SLOTS):
                load_r[w].wait()

                def set_right(s, carry):
                    high, low = split(stage_r[w, s] * mask[w * NS + s])
                    rcat[s, 0:BK, w * BK:(w + 1) * BK] = high
                    rcat[s, BK:2 * BK, w * BK:(w + 1) * BK] = low
                    return carry

                lax.fori_loop(0, NS, set_right, 0)
        else:
            for side in (0, 1):
                for copy in forward(it, side, 0):
                    copy.start()
            for i in (1, 3, 2):
                for side in (0, 1):
                    arrived(it, sector_of(i, 0) if side == 0 else sector_of(0, i), side)
                    for copy in forward(it, side, i):
                        copy.start()

            def take(q, squares):
                dx, dy = near_first(q // SIDE), near_first(q % SIDE)
                t = sector_of(dx, dy)

                @pl.when(dy != 0)
                def _():
                    arrived(it, t, 0)

                @pl.when(dx != 0)
                def _():
                    arrived(it, t, 1)

                return left_half(it, t, squares)

            squares = lax.fori_loop(0, NS, take, jnp.zeros((8, BK), F32))
            scale = scale_from(squares)
            for copy in first_hop(it):
                copy.wait_send()
            for side in (0, 1):
                for i in range(SIDE):
                    for copy in forward(it, side, i):
                        copy.wait_send()

        def give(q, total):
            dx, dy = far_first(q // SIDE), far_first(q % SIDE)
            sx, sy = (x + dx) % SIDE, (y + dy) % SIDE
            s = sx * SIDE + sy
            block = right_half(it, s, scale)
            image_parts[it, s] = block

            @pl.when(dy != 0)
            def _():
                s1_copy(it, 0, dy, sx, image_parts.at[it, s, half(0)]).start()

            @pl.when(dx != 0)
            def _():
                s1_copy(it, 1, dx, sy, image_parts.at[it, s, half(1)]).start()

            return total + fold(block * waves[it, s])

        total = lax.fori_loop(0, NS, give, jnp.zeros((8, BK), F32))
        small_start(it, 0, total * scale)
        join_map(it)
        if it + 1 < ROUNDS - 1:
            send_map(it + 1)

        def pass_on(i, carry):
            d = far_first(i)
            for side in (0, 1):
                s = sector_of(d, 0) if side == 0 else sector_of(0, d)
                chunk = (x + d) % SIDE if side == 0 else (y + d) % SIDE
                block = image_parts[it, s, half(side)]
                for e in (1, 2, 3):
                    s1_copy(it, side, e, chunk, image_parts.at[it, s, half(side)]).wait_recv()
                    block = block + r1[it, side, e - 1, chunk]
                p2[it, side, d] = block

                @pl.when(d != 0)
                def _():
                    s2_copy(it, side, d).start()

            return carry

        lax.fori_loop(0, SIDE, pass_on, 0)
        small_start(it, 1, small_sum(it, 0))
        halves = []
        for side in (0, 1):
            block = p2[it, side, 0]
            for d in (1, 2, 3):
                s2_copy(it, side, d).wait_recv()
                block = block + r2[it, side, d - 1]
            halves.append(block)
        image = jnp.concatenate(halves, axis=0)
        theta = jnp.sum(small_sum(it, 1)) / ENTRIES
        wave = waves[it, own] * scale
        wave = wave - step_size * (image - theta * wave)
        waves[it + 1, own] = wave
        if it + 1 < ITERS:
            for copy in first_hop(it + 1):
                copy.start()
        else:
            small_start(ITERS, 0, fold(wave * wave))

        for side in (0, 1):
            for d in (1, 2, 3):
                s2_copy(it, side, d).wait_send()
                for chunk in range(SIDE):
                    s1_copy(it, side, d, chunk, p2.at[it, side, d]).wait_send()
        small_end(it)

    join_map(ROUNDS - 1)
    energy = product(beside(wave.T), doubled(image))
    small_start(ITERS, 1, small_sum(ITERS, 0))
    scale = scale_from(small_sum(ITERS, 1))
    small_end(ITERS)
    wave_out[0, 0] = wave * scale
    energy = energy * (scale / BK)

    env_acc[...] = jnp.zeros((BK, BK), F32)
    for k in range(ROUNDS):
        @pl.when(seg + 2**k < NSEG)
        def _():
            s_out[k] = env_acc[...] + energy
            chain_copy(s_out, s_in, c_send, c_recv, k).start()

        @pl.when(seg >= 2**k)
        def _():
            chain_copy(s_out, s_in, c_send, c_recv, k).wait_recv()
            half_way = product(beside(s_in[k]), qdup[k])
            env_acc[...] += product(qt[k], doubled(half_way))

    env_out[0, 0] = env_acc[...]
    for k in range(ROUNDS):
        @pl.when(seg + 2**k < NSEG)
        def _():
            chain_copy(s_out, s_in, c_send, c_recv, k).wait_send()


def shards(wave_in, env_left, env_right, sector_charge, term_charge, term_live, transfer):
    smem = pl.BlockSpec(memory_space=pltpu.SMEM)
    vmem = pl.BlockSpec(memory_space=pltpu.VMEM)
    hbm = pl.BlockSpec(memory_space=pl.ANY)
    dma = pltpu.SemaphoreType.DMA
    block = jax.ShapeDtypeStruct((1, 1, BK, BK), F32)
    return pl.pallas_call(
        kernel,
        out_shape=(block, block),
        in_specs=[smem, smem, smem, hbm, hbm, hbm, hbm],
        out_specs=(vmem, vmem),
        scratch_shapes=[
            pltpu.SMEM((NS,), jnp.int32),
            pltpu.SMEM((NS,), jnp.int32),
            pltpu.SMEM((SLOTS * NS,), jnp.int32),
            pltpu.SMEM((SLOTS * NS,), jnp.int32),
            pltpu.SMEM((SLOTS * NS,), F32),
            pltpu.VMEM((SLOTS, NS, BK, BK), F32),
            pltpu.VMEM((SLOTS, NS, BK, BK), F32),
            pltpu.VMEM((NS, BK, BK), F32),
            pltpu.VMEM((BK, BK), F32),
            pltpu.VMEM((SLOTS, NS, BK, 2 * BK), BF16),
            pltpu.VMEM((NS, 2 * BK, SLOTS * BK), BF16),
            pltpu.VMEM((SLOTS, NS, 2 * BK, BK), BF16),
            pltpu.VMEM((ITERS + 1, NS, BK, BK), F32),
            pltpu.VMEM((ITERS, NS, BK, BK), F32),
            pltpu.VMEM((ITERS, 2, SIDE - 1, SIDE, HALF, BK), F32),
            pltpu.VMEM((ITERS, 2, SIDE, HALF, BK), F32),
            pltpu.VMEM((ITERS, 2, SIDE - 1, HALF, BK), F32),
            pltpu.VMEM((ITERS + 1, 2, 8, BK), F32),
            pltpu.VMEM((ITERS + 1, 2, SIDE - 1, 8, BK), F32),
            pltpu.VMEM((ROUNDS, BK, BK), F32),
            pltpu.VMEM((ROUNDS - 1, BK, BK), F32),
            pltpu.VMEM((ROUNDS, 2 * BK, 2 * BK), BF16),
            pltpu.VMEM((ROUNDS, BK, 2 * BK), BF16),
            pltpu.VMEM((ROUNDS, BK, BK), F32),
            pltpu.VMEM((ROUNDS, BK, BK), F32),
            pltpu.VMEM((BK, BK), F32),
            dma((2 + 2 * SLOTS,)),
            dma((2, SIDE - 1, SIDE)),
            dma((2, SIDE - 1, SIDE)),
            dma((2, SIDE - 1)),
            dma((2, SIDE - 1)),
            dma((2, SIDE - 1)),
            dma((2, SIDE, SIDE - 1)),
            dma((NS, 2)),
            dma((ITERS + 1, 2, SIDE - 1)),
            dma((ITERS + 1, 2, SIDE - 1)),
            dma((ROUNDS - 1,)),
            dma((ROUNDS - 1,)),
            dma((ROUNDS,)),
            dma((ROUNDS,)),
        ],
        compiler_params=pltpu.CompilerParams(
            collective_id=0, has_side_effects=True, vmem_limit_bytes=56 * 1024 * 1024
        ),
    )(sector_charge, term_charge, term_live, wave_in, env_left, env_right, transfer)


def solution(mesh):
    in_specs = (
        P("seg", None, None, None),
        P("seg", "term", None, None, None),
        P("seg", "term", None, None, None),
        P(),
        P("term", None),
        P("term"),
        P("seg", None, None, None),
    )
    out_specs = (P("seg", "term", None, None), P("seg", "term", None, None))
    return jax.shard_map(shards, mesh=mesh, in_specs=in_specs, out_specs=out_specs, check_vma=False)
```

time: 646 us -> 103 us (0.16)
  the two profiles are of different devices: /device:TPU:1 before, /device:TPU:224 now
where the time goes in v1:
time: 103 us
  Pallas kernels  96.8 us (94%)
  local copies, waits for them, and re-layouts  5.63 us (5%)
    pallas_call x1, Pallas kernels, shards(): pl.pallas_call(kernel, out_shape=(block, block), in_specs=[smem, smem, sm...  96.8 us
    unnamed x4, local copies, waits for them, and re-layouts  5.63 us

profile of v1, /device:TPU:224, one launch (start us, length us, event | category | flops | bytes accessed | tf_op | source)
XLA Modules:
  0.0 103.1 jit_solution(4808443944906063380)
XLA Ops:
  0.6 1.3 %copy.10.term_ref = s32[4,2]{1,0:T(4,128)} copy(s32[4,2]{0,1:T(2,128)} %param.11) | data formatting | bytes 64 | tf_op args[4]
  2.0 1.4 %copy.9.sector_ref = s32[16,2]{1,0:T(8,128)} copy(s32[16,2]{0,1:T(2,128)} %param.10) | data formatting | bytes 256 | tf_op args[3]
  3.3 96.8 %shard_map.86 = (f32[1,1,128,128]{3,2,1,0:T(8,128)}, f32[1,1,128,128]{3,2,1,0:T(8,128)}) custom-call(s32[16,2]{1,0:T(8,128)} %copy.9.sector_ref, s32[4,2]{1,0:T(4,128)} %copy.10.term_ref, s32[4]{0:T(128)} %live_ref.1, f32[1,16,128,128]{3,2,1,0:T(8,128)} %wave_hbm.1, f32[1,4,16,128,128]{4,3,2,1,0:T(8,128)} %left_hbm.1, f32[1,4,16,128,128]{4,3,2,1,0:T(8,128)} %right_hbm.1, ...), custom_call_target="tpu_custom_call" | custom-call | tf_op jit(solution)/shard_map/pallas_call | solution.py:419
  100.1 1.5 %copy.13 = f32[1,1,128,128]{3,2,1,0:T(8,128)} copy(f32[1,1,128,128]{3,2,1,0:T(8,128)} %get-tuple-element.4) | data formatting | bytes 131072
  101.6 1.5 %copy.14 = f32[1,1,128,128]{3,2,1,0:T(8,128)} copy(f32[1,1,128,128]{3,2,1,0:T(8,128)} %get-tuple-element.5) | data formatting | bytes 131072

commit v2 on v1

v2 whole, which is shorter than its diff:
```python
import functools

import jax
import jax.numpy as jnp
from jax import lax
from jax.experimental import pallas as pl
from jax.experimental.pallas import tpu as pltpu
from jax.sharding import PartitionSpec as P

ITERS = 3
SIDE = 4
CHARGES = 4
BK = 128
HALF = 64
NS = 16
SLOTS = 4
NSEG = 16
CHIPS = NSEG // 2
ENTRIES = float(NS * BK * BK)
mean_eps = 1e-06
step_size = 0.5

F32 = jnp.float32
BF16 = jnp.bfloat16
MESH = pl.DeviceIdType.MESH


def split(x):
    high = x.astype(BF16)
    low = (x - high.astype(F32)).astype(BF16)
    return high, low


def beside(x):
    return jnp.concatenate(split(x), axis=1)


def doubled(x):
    row = beside(x)
    return jnp.concatenate([row, row], axis=0)


def product(left, right):
    both = jnp.dot(left, right, preferred_element_type=F32)
    return both[:, :BK] + both[:, BK:]


def fold(x):
    return jnp.sum(x.reshape(x.shape[0] // 8, 8, x.shape[1]), axis=0)


def far_first(i):
    return (2 + i + i // 2 + 2 * (i // 3)) % 4


def near_first(i):
    return i + i // 2 - 2 * (i // 3)


def by_shells(q):
    past = [(q + 9) // 16, (q + 4) // 16, (q + 1) // 16]
    r = past[0] + past[1] + past[2]
    m = q - 7 * past[0] - 5 * past[1] - 3 * past[2]
    below = (m + 4 + r) // 8
    return r + below * (m - 3 + r), r + (1 - below) * m


def kernel(
    sector_ref, term_ref, live_ref, wave_hbm, left_hbm, right_hbm, transfer_hbm,
    out,
    code, place, source, target, mask,
    stage_l, stage_r, stage_t, lcat, rcat, inner, waves, image_parts, images,
    r1, p2, r2, small, small_in, norm_out, norm_in,
    t_out, t_in, pair_out, pair_in, tdup, tt, wdup, wt, e_out, e_in, c_out, c_in, f_out, f_in, n_out, n_in,
    load_sem, s1_send, s1_recv, s2_send, s2_recv, g1_send, g2_send, g_recv,
    small_send, small_recv, norm_send, norm_recv, core_send, core_recv, pair_send, pair_recv, f_send, f_recv,
):
    seg = lax.axis_index("seg")
    own = lax.axis_index("term")
    x, y = own // SIDE, own % SIDE
    z, core = seg // 2, seg % 2

    def at(dx, dy):
        return (seg, ((x + dx) % SIDE) * SIDE + (y + dy) % SIDE)

    other_core = (seg + 1 - 2 * core, own)

    load_w = pltpu.make_async_copy(wave_hbm.at[0], waves.at[0], load_sem.at[0])
    load_t = pltpu.make_async_copy(transfer_hbm.at[0, own], stage_t, load_sem.at[1])
    load_w.start()
    load_t.start()
    load_l = [pltpu.make_async_copy(left_hbm.at[0, w], stage_l.at[w], load_sem.at[2 + w]) for w in range(SLOTS)]
    load_r = [pltpu.make_async_copy(right_hbm.at[0, w], stage_r.at[w], load_sem.at[6 + w]) for w in range(SLOTS)]
    for load in load_l + load_r:
        load.start()
    barrier = pltpu.get_barrier_semaphore()
    others = [(dx, dy) for dx in (2, 1, 3, 0) for dy in (2, 1, 3, 0) if (dx, dy) != (0, 0)]
    for dx, dy in others:
        pl.semaphore_signal(barrier, inc=1, device_id=at(dx, dy), device_id_type=MESH)
    for d in range(1, CHIPS):
        pl.semaphore_signal(barrier, inc=1, device_id=((seg + 2 * d) % NSEG, own), device_id_type=MESH)
    pl.semaphore_signal(barrier, inc=1, device_id=other_core, device_id_type=MESH)
    greeted = len(others) + CHIPS

    for s in range(NS):
        code[s] = sector_ref[0, s] * CHARGES + sector_ref[1, s]

    def find(c, carry):
        found = jnp.int32(0)
        for s in range(NS):
            found = jnp.where(code[s] == c, jnp.int32(s), found)
        place[c] = found
        return carry

    lax.fori_loop(0, NS, find, 0)

    def look_up(w, carry):
        up_change, down_change = term_ref[0, w], term_ref[1, w]
        alive = live_ref[w].astype(F32)

        def one(s, carry):
            def sector_at(up, down):
                inside = (up >= 0) & (up < CHARGES) & (down >= 0) & (down < CHARGES)
                return inside, place[jnp.where(inside, up * CHARGES + down, 0)]

            up, down = sector_ref[0, s], sector_ref[1, s]
            inside, found = sector_at(up - up_change, down - down_change)
            source[w * NS + s] = found
            mask[w * NS + s] = jnp.where(inside, alive, jnp.float32(0))
            target[w * NS + s] = sector_at(up + up_change, down + down_change)[1]
            return carry

        return lax.fori_loop(0, NS, one, carry)

    lax.fori_loop(0, SLOTS, look_up, 0)

    load_w.wait()

    def add_square(t, total):
        v = waves[0, t]
        return total + fold(v * v)

    def scale_from(squares):
        return lax.rsqrt(jnp.sum(squares) / ENTRIES + mean_eps)

    zero = jnp.zeros((8, BK), F32)
    squares = lax.fori_loop(0, NS, add_square, zero, unroll=2)
    scale = scale_from(squares)

    for w in range(SLOTS):
        load_l[w].wait()

        def set_left(s, carry):
            lcat[w, s] = beside(stage_l[w, s])
            return carry

        lax.fori_loop(0, NS, set_left, 0, unroll=2)

    def core_copy(src, dst, k):
        return pltpu.make_async_remote_copy(
            src_ref=src, dst_ref=dst, send_sem=core_send.at[k], recv_sem=core_recv.at[k],
            device_id=other_core, device_id_type=MESH,
        )

    def up_copy(src, dst, send, recv, d):
        return pltpu.make_async_remote_copy(
            src_ref=src, dst_ref=dst.at[d - 1], send_sem=send.at[d - 1], recv_sem=recv.at[d - 1],
            device_id=((seg + 2 * d) % NSEG, own), device_id_type=MESH,
        )

    load_t.wait()
    rows = lax.broadcasted_iota(jnp.int32, (BK, BK), 0)
    columns = lax.broadcasted_iota(jnp.int32, (BK, BK), 1)
    t_out[...] = stage_t[...] + jnp.where(rows == columns, jnp.float32(1), jnp.float32(0))
    pl.semaphore_wait(barrier, greeted)

    @pl.when(core == 0)
    def _():
        core_copy(t_out, t_in, 0).start()

    def set_map(d, value):
        wdup[d - 1] = doubled(value)
        wt[d - 1] = beside(value.T)

    def chain_step(it):
        @pl.when(core == 1)
        def _():
            if it == 0:
                own_map = t_out[...]
                tdup[...] = doubled(own_map)
                tt[...] = beside(own_map.T)
                core_copy(t_out, t_in, 0).wait_recv()
                lower_map = t_in[...]
                set_map(1, lower_map)
                pair_out[...] = product(beside(lower_map), tdup[...])
                for d in range(1, CHIPS - 1):
                    @pl.when((z >= 1) & (z + d < CHIPS))
                    def _():
                        up_copy(pair_out, pair_in, pair_send, pair_recv, d).start()
            else:
                for d in ((2, 3, 4) if it == 1 else (5, 6, 7)):
                    @pl.when(z >= d)
                    def _():
                        up_copy(pair_out, pair_in, pair_send, pair_recv, d - 1).wait_recv()
                        set_map(d, product(beside(pair_in[d - 2]), wdup[d - 2]))

    def s1_copy(it, side, d, chunk, src):
        return pltpu.make_async_remote_copy(
            src_ref=src, dst_ref=r1.at[it, side, d - 1, chunk],
            send_sem=s1_send.at[side, d - 1, chunk], recv_sem=s1_recv.at[side, d - 1, chunk],
            device_id=at(0, d) if side == 0 else at(d, 0), device_id_type=MESH,
        )

    def s2_copy(it, side, d):
        return pltpu.make_async_remote_copy(
            src_ref=p2.at[it, side, d], dst_ref=r2.at[it, side, d - 1],
            send_sem=s2_send.at[side, d - 1], recv_sem=s2_recv.at[side, d - 1],
            device_id=at(d, 0) if side == 0 else at(0, d), device_id_type=MESH,
        )

    def half(side):
        return pl.ds(side * HALF, HALF)

    def small_copy(it, side, d):
        return pltpu.make_async_remote_copy(
            src_ref=small.at[it, side], dst_ref=small_in.at[it, side, d - 1],
            send_sem=small_send.at[it, side, d - 1], recv_sem=small_recv.at[it, side, d - 1],
            device_id=at(0, d) if side == 0 else at(d, 0), device_id_type=MESH,
        )

    def small_start(it, side, value):
        small[it, side] = value
        for d in (2, 1, 3):
            small_copy(it, side, d).start()

    def small_sum(it, side):
        total = small[it, side]
        for d in (1, 2, 3):
            small_copy(it, side, d).wait_recv()
            total = total + small_in[it, side, d - 1]
        return total

    def small_end(it):
        for side in (0, 1):
            for d in (1, 2, 3):
                small_copy(it, side, d).wait_send()

    def norm_copy(dx, dy):
        slot = dx * SIDE + dy
        return pltpu.make_async_remote_copy(
            src_ref=norm_out, dst_ref=norm_in.at[slot], send_sem=norm_send.at[slot], recv_sem=norm_recv.at[slot],
            device_id=at(dx, dy), device_id_type=MESH,
        )

    def gather_copy(it, sector, side, send, device):
        block = images.at[it, sector, half(side)]
        return pltpu.make_async_remote_copy(
            src_ref=block, dst_ref=block, send_sem=send, recv_sem=g_recv.at[sector, side],
            device_id=device, device_id_type=MESH,
        )

    def arrived(it, sector, side):
        gather_copy(it, sector, side, g1_send.at[0, 0], at(1, 0)).wait_recv()

    def sector_of(dx, dy):
        return ((x + dx) % SIDE) * SIDE + (y + dy) % SIDE

    def forward(it, side, i):
        sector = sector_of(i, 0) if side == 0 else sector_of(0, i)
        return [
            gather_copy(it, sector, side, g2_send.at[side, i, d - 1], at(0, d) if side == 0 else at(d, 0))
            for d in (2, 1, 3)
        ]

    def first_hop(it):
        return [
            gather_copy(it, own, side, g1_send.at[side, d - 1], at(d, 0) if side == 0 else at(0, d))
            for d in (2, 1, 3) for side in (0, 1)
        ]

    def left_half(t, v):
        left = jnp.concatenate([lcat[w, target[w * NS + t]] for w in range(SLOTS)], axis=0)
        high, low = split(product(left, doubled(v)))
        for w in range(SLOTS):
            part = slice(w * BK, (w + 1) * BK)
            inner[w, t] = jnp.concatenate([high[part], low[part]], axis=0)

    def right_half(s, scale):
        left = jnp.concatenate([inner[w, source[w * NS + s]] for w in range(SLOTS)], axis=1)
        both = lax.dot_general(left, rcat[s], (((1,), (1,)), ((), ())), preferred_element_type=F32)
        return (both[:BK, :BK] + both[:BK, BK:] + both[BK:, :BK] + both[BK:, BK:]) * scale

    for it in range(ITERS):
        if it == 0:
            def begin(t, carry):
                v = waves[0, t] * scale
                waves[0, t] = v
                left_half(t, v)
                return carry

            lax.fori_loop(0, NS, begin, 0, unroll=2)
            scale = jnp.float32(1)
            for w in range(SLOTS):
                load_r[w].wait()

                def set_right(s, carry):
                    high, low = split(stage_r[w, s] * mask[w * NS + s])
                    rcat[s, 0:BK, w * BK:(w + 1) * BK] = high
                    rcat[s, BK:2 * BK, w * BK:(w + 1) * BK] = low
                    return carry

                lax.fori_loop(0, NS, set_right, 0, unroll=2)
        else:
            for side in (0, 1):
                for copy in forward(it - 1, side, 0):
                    copy.start()
            for i in (1, 3, 2):
                for side in (0, 1):
                    arrived(it - 1, sector_of(i, 0) if side == 0 else sector_of(0, i), side)
                    for copy in forward(it - 1, side, i):
                        copy.start()
            theta = jnp.sum(small_sum(it - 1, 1)) / ENTRIES

            def take(p, squares):
                blocks = []
                for q in (2 * p, 2 * p + 1):
                    dx, dy = near_first(q // SIDE), near_first(q % SIDE)
                    t = sector_of(dx, dy)
                    blocks.append(t)

                    @pl.when(dy != 0)
                    def _():
                        arrived(it - 1, t, 0)

                    @pl.when(dx != 0)
                    def _():
                        arrived(it - 1, t, 1)

                values = []
                for t in blocks:
                    wave = waves[it - 1, t] * scale
                    values.append(wave - step_size * (images[it - 1, t] - theta * wave))
                for t, v in zip(blocks, values):
                    left_half(t, v)
                for t, v in zip(blocks, values):
                    waves[it, t] = v
                    squares = squares + fold(v * v)
                return squares

            squares = lax.fori_loop(0, NS // 2, take, zero)
            scale = scale_from(squares)
            for copy in first_hop(it - 1):
                copy.wait_send()
            for side in (0, 1):
                for i in range(SIDE):
                    for copy in forward(it - 1, side, i):
                        copy.wait_send()
            small_end(it - 1)

        def give(p, total):
            places = []
            for q in (2 * p, 2 * p + 1):
                i, k = by_shells(q)
                places.append((far_first(i), far_first(k)))
            made = []
            for dx, dy in places:
                made.append(right_half(sector_of(dx, dy), scale))
            for (dx, dy), block in zip(places, made):
                image_parts[it, sector_of(dx, dy)] = block
            for (dx, dy), block in zip(places, made):
                sx, sy = (x + dx) % SIDE, (y + dy) % SIDE
                s = sx * SIDE + sy

                @pl.when(dy != 0)
                def _():
                    s1_copy(it, 0, dy, sx, image_parts.at[it, s, half(0)]).start()

                @pl.when(dx != 0)
                def _():
                    s1_copy(it, 1, dx, sy, image_parts.at[it, s, half(1)]).start()

                total = total + fold(block * waves[it, s])
            return total

        total = lax.fori_loop(0, NS // 2, give, zero)
        small_start(it, 0, total * scale)
        chain_step(it)

        def pass_on(i, carry):
            d = far_first(i)
            for side in (0, 1):
                s = sector_of(d, 0) if side == 0 else sector_of(0, d)
                chunk = (x + d) % SIDE if side == 0 else (y + d) % SIDE
                block = image_parts[it, s, half(side)]
                for e in (1, 2, 3):
                    s1_copy(it, side, e, chunk, image_parts.at[it, s, half(side)]).wait_recv()
                    block = block + r1[it, side, e - 1, chunk]
                p2[it, side, d] = block

                @pl.when(d != 0)
                def _():
                    s2_copy(it, side, d).start()

            return carry

        lax.fori_loop(0, SIDE, pass_on, 0)
        small_start(it, 1, small_sum(it, 0))
        halves = []
        for side in (0, 1):
            block = p2[it, side, 0]
            for d in (1, 2, 3):
                s2_copy(it, side, d).wait_recv()
                block = block + r2[it, side, d - 1]
            halves.append(block)
        image = jnp.concatenate(halves, axis=0)
        if it + 1 < ITERS:
            images[it, own] = image
            for copy in first_hop(it):
                copy.start()
        else:
            theta = jnp.sum(small_sum(it, 1)) / ENTRIES
            wave = waves[it, own] * scale
            wave = wave - step_size * (image - theta * wave)
            norm_out[...] = fold(wave * wave)
            for dx, dy in others:
                norm_copy(dx, dy).start()

        for side in (0, 1):
            for d in (1, 2, 3):
                s2_copy(it, side, d).wait_send()
                for chunk in range(SIDE):
                    s1_copy(it, side, d, chunk, p2.at[it, side, d]).wait_send()

    energy = product(beside(wave.T), doubled(image))

    @pl.when(core == 0)
    def _():
        e_out[...] = energy
        core_copy(e_out, e_in, 1).start()

    @pl.when(core == 1)
    def _():
        core_copy(e_out, e_in, 1).wait_recv()
        n_out[...] = product(tt[...], doubled(product(beside(e_in[...]), tdup[...])))

    squares = norm_out[...]
    for dx, dy in others:
        norm_copy(dx, dy).wait_recv()
        squares = squares + norm_in[dx * SIDE + dy]
    scale = scale_from(squares)
    energy_scale = scale / BK

    @pl.when(core == 0)
    def _():
        c_out[...] = jnp.full((8, BK), energy_scale, F32)
        core_copy(c_out, c_in, 2).start()

    out[0] = wave * scale

    @pl.when(core == 1)
    def _():
        core_copy(c_out, c_in, 2).wait_recv()
        lower = n_out[...] * c_in[0:1, 0:1]
        f_out[...] = energy * energy_scale + lower
        for d in range(CHIPS - 1, 0, -1):
            @pl.when(z + d < CHIPS)
            def _():
                up_copy(f_out, f_in, f_send, f_recv, d).start()

        out[1] = lower
        n_out[...] = jnp.zeros((BK, BK), F32)
        for d in range(1, CHIPS):
            @pl.when(z >= d)
            def _():
                up_copy(f_out, f_in, f_send, f_recv, d).wait_recv()
                n_out[...] += product(wt[d - 1], doubled(product(beside(f_in[d - 1]), wdup[d - 1])))

        core_copy(n_out, n_in, 3).start()
        out[1] += product(tt[...], doubled(product(beside(n_out[...]), tdup[...])))
        for d in range(1, CHIPS):
            @pl.when(z + d < CHIPS)
            def _():
                up_copy(f_out, f_in, f_send, f_recv, d).wait_send()

            if d < CHIPS - 1:
                @pl.when((z >= 1) & (z + d < CHIPS))
                def _():
                    up_copy(pair_out, pair_in, pair_send, pair_recv, d).wait_send()

        core_copy(n_out, n_in, 3).wait_send()

    @pl.when(core == 0)
    def _():
        core_copy(t_out, t_in, 0).wait_send()
        core_copy(e_out, e_in, 1).wait_send()
        core_copy(c_out, c_in, 2).wait_send()
        core_copy(n_out, n_in, 3).wait_recv()
        out[1] = n_in[...]

    for dx, dy in others:
        norm_copy(dx, dy).wait_send()
    small_end(ITERS - 1)


def shards(wave_in, env_left, env_right, sector_charge, term_charge, term_live, transfer):
    smem = pl.BlockSpec(memory_space=pltpu.SMEM)
    vmem = pl.BlockSpec(memory_space=pltpu.VMEM)
    hbm = pl.BlockSpec(memory_space=pl.ANY)
    dma = pltpu.SemaphoreType.DMA
    square = pltpu.VMEM((BK, BK), F32)
    tile = pltpu.VMEM((8, BK), F32)
    both = pl.pallas_call(
        kernel,
        out_shape=jax.ShapeDtypeStruct((2, BK, BK), F32),
        in_specs=[smem, smem, smem, hbm, hbm, hbm, hbm],
        out_specs=vmem,
        scratch_shapes=[
            pltpu.SMEM((NS,), jnp.int32),
            pltpu.SMEM((NS,), jnp.int32),
            pltpu.SMEM((SLOTS * NS,), jnp.int32),
            pltpu.SMEM((SLOTS * NS,), jnp.int32),
            pltpu.SMEM((SLOTS * NS,), F32),
            pltpu.VMEM((SLOTS, NS, BK, BK), F32),
            pltpu.VMEM((SLOTS, NS, BK, BK), F32),
            square,
            pltpu.VMEM((SLOTS, NS, BK, 2 * BK), BF16),
            pltpu.VMEM((NS, 2 * BK, SLOTS * BK), BF16),
            pltpu.VMEM((SLOTS, NS, 2 * BK, BK), BF16),
            pltpu.VMEM((ITERS, NS, BK, BK), F32),
            pltpu.VMEM((ITERS, NS, BK, BK), F32),
            pltpu.VMEM((ITERS - 1, NS, BK, BK), F32),
            pltpu.VMEM((ITERS, 2, SIDE - 1, SIDE, HALF, BK), F32),
            pltpu.VMEM((ITERS, 2, SIDE, HALF, BK), F32),
            pltpu.VMEM((ITERS, 2, SIDE - 1, HALF, BK), F32),
            pltpu.VMEM((ITERS, 2, 8, BK), F32),
            pltpu.VMEM((ITERS, 2, SIDE - 1, 8, BK), F32),
            tile,
            pltpu.VMEM((NS, 8, BK), F32),
            square,
            square,
            square,
            pltpu.VMEM((CHIPS - 2, BK, BK), F32),
            pltpu.VMEM((2 * BK, 2 * BK), BF16),
            pltpu.VMEM((BK, 2 * BK), BF16),
            pltpu.VMEM((CHIPS - 1, 2 * BK, 2 * BK), BF16),
            pltpu.VMEM((CHIPS - 1, BK, 2 * BK), BF16),
            square,
            square,
            tile,
            tile,
            square,
            pltpu.VMEM((CHIPS - 1, BK, BK), F32),
            square,
            square,
            dma((2 + 2 * SLOTS,)),
            dma((2, SIDE - 1, SIDE)),
            dma((2, SIDE - 1, SIDE)),
            dma((2, SIDE - 1)),
            dma((2, SIDE - 1)),
            dma((2, SIDE - 1)),
            dma((2, SIDE, SIDE - 1)),
            dma((NS, 2)),
            dma((ITERS, 2, SIDE - 1)),
            dma((ITERS, 2, SIDE - 1)),
            dma((NS,)),
            dma((NS,)),
            dma((4,)),
            dma((4,)),
            dma((CHIPS - 2,)),
            dma((CHIPS - 2,)),
            dma((CHIPS - 1,)),
            dma((CHIPS - 1,)),
        ],
        compiler_params=pltpu.CompilerParams(
            collective_id=0, has_side_effects=True, vmem_limit_bytes=56 * 1024 * 1024
        ),
    )(sector_charge.T, term_charge.T, term_live, wave_in, env_left, env_right, transfer)
    block = (1, 1, BK, BK)
    return both[0].reshape(block), both[1].reshape(block)


def solution(mesh):
    in_specs = (
        P("seg", None, None, None),
        P("seg", "term", None, None, None),
        P("seg", "term", None, None, None),
        P(),
        P("term", None),
        P("term"),
        P("seg", None, None, None),
    )
    out_specs = (P("seg", "term", None, None), P("seg", "term", None, None))
    return jax.shard_map(shards, mesh=mesh, in_specs=in_specs, out_specs=out_specs, check_vma=False)
```

time: 103 us -> 89 us (0.86)
  the two profiles are of different devices: /device:TPU:224 before, /device:TPU:1 now
where the time goes in v2:
time: 89 us; the launch traced here: 88.9 us
  Pallas kernels  86.7 us (97%)
  local copies, waits for them, and re-layouts  1.53 us (2%)
    pallas_call x1, Pallas kernels, shards(): pl.pallas_call(kernel, out_shape=jax.ShapeDtypeStruct((2, BK, BK), F32),...  86.7 us

profile of v2, /device:TPU:1, one launch (start us, length us, event | category | flops | bytes accessed | tf_op | source)
XLA Modules:
  0.0 88.9 jit_solution(13151748801530060714)
XLA Ops:
  0.6 86.7 %shard_map.86 = f32[2,128,128]{2,1,0:T(8,128)} custom-call(s32[2,16]{1,0:T(2,128)} %bitcast.6, s32[2,4]{1,0:T(2,128)} %bitcast.7, s32[4]{0:T(128)} %live_ref.1, f32[1,16,128,128]{3,2,1,0:T(8,128)} %wave_hbm.1, f32[1,4,16,128,128]{4,3,2,1,0:T(8,128)} %left_hbm.1, f32[1,4,16,128,128]{4,3,2,1,0:T(8,128)} %right_hbm.1, f32[1,16,128,128]{3,2,1,0:T(8,128)} %transfer_hbm.1), custom_call_target="tpu_custom_call" | custom-call | tf_op jit(solution)/shard_map/pallas_call | solution.py:512
  87.4 1.5 %slice_bitcast_fusion = (f32[1,1,128,128]{3,2,1,0:T(8,128)}, f32[1,1,128,128]{3,2,1,0:T(8,128)}) fusion(f32[2,128,128]{2,1,0:T(8,128)} %shard_map.86), kind=kLoop, calls=%fused_computation | loop fusion | bytes 262144 | tf_op jit(solution)/shard_map/reshape;squeeze | solution.py:579

commit v3 on v2

v3 whole, which is shorter than its diff:
```python
import functools

import jax
import jax.numpy as jnp
from jax import lax
from jax.experimental import pallas as pl
from jax.experimental.pallas import tpu as pltpu
from jax.sharding import PartitionSpec as P

ITERS = 3
SIDE = 4
CHARGES = 4
BK = 128
HALF = 64
NS = 16
SLOTS = 4
NSEG = 16
CHIPS = NSEG // 2
ENTRIES = float(NS * BK * BK)
mean_eps = 1e-06
step_size = 0.5

F32 = jnp.float32
BF16 = jnp.bfloat16
MESH = pl.DeviceIdType.MESH


def split(x):
    high = x.astype(BF16)
    low = (x - high.astype(F32)).astype(BF16)
    return high, low


def beside(x):
    return jnp.concatenate(split(x), axis=1)


def doubled(x):
    row = beside(x)
    return jnp.concatenate([row, row], axis=0)


def product(left, right):
    both = jnp.dot(left, right, preferred_element_type=F32)
    return both[:, :BK] + both[:, BK:]


def fold(x):
    return jnp.sum(x.reshape(x.shape[0] // 8, 8, x.shape[1]), axis=0)


def first_shell(r):
    return [(r, k) for k in range(r, SIDE)] + [(k, r) for k in range(r + 1, SIDE)]


def last_shell(r):
    return [(r, k) for k in range(r)] + [(k, r) for k in range(r)] + [(r, r)]


def kernel(
    sector_hbm, term_hbm, live_hbm, wave_hbm, left_hbm, right_hbm, transfer_hbm,
    out,
    sector_ref, term_ref, live_ref, code, place, source, target, mask,
    stage_l, stage_r, stage_t, lcat, rcat, inner, waves, image_parts, images,
    r1, p2, r2, small, small_in, norm_out, norm_in,
    t_out, t_in, pair_out, pair_in, tdup, tt, wdup, wt, e_out, e_in, c_out, c_in, f_out, f_in, n_out, n_in,
    load_sem, s1_send, s1_recv, s2_send, s2_recv, g_send, g_recv,
    small_send, small_recv, norm_send, norm_recv, core_send, core_recv, pair_send, pair_recv, f_send, f_recv,
):
    seg = lax.axis_index("seg")
    own = lax.axis_index("term")
    x, y = own // SIDE, own % SIDE
    z, core = seg // 2, seg % 2

    def at(dx, dy):
        return (seg, ((x + dx) % SIDE) * SIDE + (y + dy) % SIDE)

    other_core = (seg + 1 - 2 * core, own)

    load_w = pltpu.make_async_copy(wave_hbm.at[0], waves.at[0], load_sem.at[0])
    load_t = pltpu.make_async_copy(transfer_hbm.at[0, own], stage_t, load_sem.at[1])
    load_i = [
        pltpu.make_async_copy(sector_hbm, sector_ref, load_sem.at[10]),
        pltpu.make_async_copy(term_hbm, term_ref, load_sem.at[11]),
        pltpu.make_async_copy(live_hbm, live_ref, load_sem.at[12]),
    ]
    for load in load_i:
        load.start()
    load_w.start()
    load_t.start()
    load_l = [pltpu.make_async_copy(left_hbm.at[0, w], stage_l.at[w], load_sem.at[2 + w]) for w in range(SLOTS)]
    load_r = [pltpu.make_async_copy(right_hbm.at[0, w], stage_r.at[w], load_sem.at[6 + w]) for w in range(SLOTS)]
    for load in load_l + load_r:
        load.start()
    barrier = pltpu.get_barrier_semaphore()
    others = [(dx, dy) for dx in (2, 1, 3, 0) for dy in (2, 1, 3, 0) if (dx, dy) != (0, 0)]
    for dx, dy in others:
        pl.semaphore_signal(barrier, inc=1, device_id=at(dx, dy), device_id_type=MESH)
    for d in range(1, CHIPS):
        pl.semaphore_signal(barrier, inc=1, device_id=((seg + 2 * d) % NSEG, own), device_id_type=MESH)
    pl.semaphore_signal(barrier, inc=1, device_id=other_core, device_id_type=MESH)
    greeted = len(others) + CHIPS

    for load in load_i:
        load.wait()
    for s in range(NS):
        code[s] = sector_ref[0, s] * CHARGES + sector_ref[1, s]

    def find(c, carry):
        found = jnp.int32(0)
        for s in range(NS):
            found = jnp.where(code[s] == c, jnp.int32(s), found)
        place[c] = found
        return carry

    lax.fori_loop(0, NS, find, 0)

    def look_up(w, carry):
        up_change, down_change = term_ref[0, w], term_ref[1, w]
        alive = live_ref[w].astype(F32)

        def one(s, carry):
            def sector_at(up, down):
                inside = (up >= 0) & (up < CHARGES) & (down >= 0) & (down < CHARGES)
                return inside, place[jnp.where(inside, up * CHARGES + down, 0)]

            up, down = sector_ref[0, s], sector_ref[1, s]
            inside, found = sector_at(up - up_change, down - down_change)
            source[w * NS + s] = found
            mask[w * NS + s] = jnp.where(inside, alive, jnp.float32(0))
            target[w * NS + s] = sector_at(up + up_change, down + down_change)[1]
            return carry

        return lax.fori_loop(0, NS, one, carry)

    lax.fori_loop(0, SLOTS, look_up, 0)

    load_w.wait()

    def add_square(t, total):
        v = waves[0, t]
        return total + fold(v * v)

    def scale_from(squares):
        return lax.rsqrt(jnp.sum(squares) / ENTRIES + mean_eps)

    zero = jnp.zeros((8, BK), F32)
    squares = lax.fori_loop(0, NS, add_square, zero, unroll=2)
    scale = scale_from(squares)

    for w in range(SLOTS):
        load_l[w].wait()

        def set_left(s, carry):
            lcat[w, s] = beside(stage_l[w, s])
            return carry

        lax.fori_loop(0, NS, set_left, 0, unroll=2)

    def core_copy(src, dst, k):
        return pltpu.make_async_remote_copy(
            src_ref=src, dst_ref=dst, send_sem=core_send.at[k], recv_sem=core_recv.at[k],
            device_id=other_core, device_id_type=MESH,
        )

    def up_copy(src, dst, send, recv, d):
        return pltpu.make_async_remote_copy(
            src_ref=src, dst_ref=dst.at[d - 1], send_sem=send.at[d - 1], recv_sem=recv.at[d - 1],
            device_id=((seg + 2 * d) % NSEG, own), device_id_type=MESH,
        )

    load_t.wait()
    rows = lax.broadcasted_iota(jnp.int32, (BK, BK), 0)
    columns = lax.broadcasted_iota(jnp.int32, (BK, BK), 1)
    t_out[...] = stage_t[...] + jnp.where(rows == columns, jnp.float32(1), jnp.float32(0))
    pl.semaphore_wait(barrier, greeted)

    @pl.when(core == 0)
    def _():
        core_copy(t_out, t_in, 0).start()

    def set_map(d, value):
        wdup[d - 1] = doubled(value)
        wt[d - 1] = beside(value.T)

    def first_maps():
        @pl.when(core == 1)
        def _():
            own_map = t_out[...]
            tdup[...] = doubled(own_map)
            tt[...] = beside(own_map.T)
            core_copy(t_out, t_in, 0).wait_recv()
            lower_map = t_in[...]
            set_map(1, lower_map)
            pair_out[...] = product(beside(lower_map), tdup[...])
            for d in range(1, CHIPS - 1):
                @pl.when((z >= 1) & (z + d < CHIPS))
                def _():
                    up_copy(pair_out, pair_in, pair_send, pair_recv, d).start()

    def more_maps(which):
        for d in which:
            @pl.when((core == 1) & (z >= d))
            def _():
                up_copy(pair_out, pair_in, pair_send, pair_recv, d - 1).wait_recv()
                set_map(d, product(beside(pair_in[d - 2]), wdup[d - 2]))

    def half(side):
        return pl.ds(side * HALF, HALF)

    def along(side, d):
        return at(0, d) if side == 0 else at(d, 0)

    def s1_copy(it, side, d, chunk):
        sector = chunk * SIDE + (y + d) % SIDE if side == 0 else ((x + d) % SIDE) * SIDE + chunk
        return pltpu.make_async_remote_copy(
            src_ref=image_parts.at[it, sector, half(side)], dst_ref=r1.at[it, side, d - 1, chunk],
            send_sem=s1_send.at[0], recv_sem=s1_recv.at[chunk],
            device_id=along(side, d), device_id_type=MESH,
        )

    def s2_copy(it, side, d, chunk, slot):
        return pltpu.make_async_remote_copy(
            src_ref=p2.at[it, side, chunk], dst_ref=r2.at[it, side, d - 1, slot],
            send_sem=s2_send.at[0], recv_sem=s2_recv.at[slot],
            device_id=along(1 - side, d), device_id_type=MESH,
        )

    def on_line(side, chunk):
        return chunk * SIDE + y if side == 0 else x * SIDE + chunk

    def gather_copy(it, side, d, chunk):
        block = images.at[it, on_line(side, chunk), half(side)]
        return pltpu.make_async_remote_copy(
            src_ref=block, dst_ref=block, send_sem=g_send.at[0], recv_sem=g_recv.at[chunk],
            device_id=along(side, d), device_id_type=MESH,
        )

    def wait_for(ref, sem):
        pltpu.make_async_copy(ref, ref, sem).wait()

    def small_copy(it, side, d):
        return pltpu.make_async_remote_copy(
            src_ref=small.at[it, side], dst_ref=small_in.at[it, side, d - 1],
            send_sem=small_send.at[side], recv_sem=small_recv.at[side],
            device_id=along(side, d), device_id_type=MESH,
        )

    def small_start(it, side, value):
        small[it, side] = value
        for d in (2, 1, 3):
            small_copy(it, side, d).start()

    def small_sum(it, side):
        wait_for(small_in.at[it, side], small_recv.at[side])
        return small[it, side] + small_in[it, side, 0] + small_in[it, side, 1] + small_in[it, side, 2]

    def small_end(it):
        for side in (0, 1):
            wait_for(small_in.at[it, side], small_send.at[side])

    def norm_copy(dx, dy):
        return pltpu.make_async_remote_copy(
            src_ref=norm_out, dst_ref=norm_in.at[dx * SIDE + dy - 1], send_sem=norm_send.at[0], recv_sem=norm_recv.at[0],
            device_id=at(dx, dy), device_id_type=MESH,
        )

    def left_half(t, v):
        left = jnp.concatenate([lcat[w, target[w * NS + t]] for w in range(SLOTS)], axis=0)
        high, low = split(product(left, doubled(v)))
        for w in range(SLOTS):
            part = slice(w * BK, (w + 1) * BK)
            inner[w, t] = jnp.concatenate([high[part], low[part]], axis=0)

    def right_half(s, scale):
        left = jnp.concatenate([inner[w, source[w * NS + s]] for w in range(SLOTS)], axis=1)
        both = lax.dot_general(left, rcat[s], (((1,), (1,)), ((), ())), preferred_element_type=F32)
        return (both[:BK, :BK] + both[:BK, BK:] + both[BK:, :BK] + both[BK:, BK:]) * scale

    for it in range(ITERS):
        if it == 0:
            def begin(t, carry):
                v = waves[0, t] * scale
                waves[0, t] = v
                left_half(t, v)
                return carry

            lax.fori_loop(0, NS, begin, 0, unroll=4)
            scale = jnp.float32(1)
            for w in range(SLOTS):
                load_r[w].wait()

                def set_right(s, carry):
                    high, low = split(stage_r[w, s] * mask[w * NS + s])
                    rcat[s, 0:BK, w * BK:(w + 1) * BK] = high
                    rcat[s, BK:2 * BK, w * BK:(w + 1) * BK] = low
                    return carry

                lax.fori_loop(0, NS, set_right, 0, unroll=2)
        else:
            theta = jnp.sum(small_sum(it - 1, 1)) / ENTRIES

            squares = zero
            for chunk in range(SIDE):
                wait_for(r1.at[it - 1, :, :, chunk], g_recv.at[chunk])
                blocks = [sx * SIDE + sy for sx, sy in last_shell(chunk)]
                for t in blocks:
                    wave = waves[it - 1, t] * scale
                    wave = wave - step_size * (images[it - 1, t] - theta * wave)
                    left_half(t, wave)
                    waves[it, t] = wave
                    squares = squares + fold(wave * wave)
            scale = scale_from(squares)
            wait_for(r1.at[it - 1], g_send.at[0])
            small_end(it - 1)

        total = zero
        for chunk in range(SIDE):
            blocks = [sx * SIDE + sy for sx, sy in first_shell(chunk)]
            for s in blocks:
                block = right_half(s, scale)
                image_parts[it, s] = block
                total = total + fold(block * waves[it, s])
            for d in (2, 1, 3):
                for side in (0, 1):
                    s1_copy(it, side, d, chunk).start()
        small_start(it, 0, total * scale)
        if it == 0:
            first_maps()
        else:
            more_maps((3, 4) if it == 1 else (6, 7))

        for chunk in range(SIDE):
            wait_for(r1.at[it, :, :, chunk], s1_recv.at[chunk])
            for side in (0, 1):
                block = image_parts[it, on_line(side, chunk), half(side)]
                for e in range(SIDE - 1):
                    block = block + r1[it, side, e, chunk]
                p2[it, side, chunk] = block
                if it + 1 < ITERS:
                    for d in (2, 1, 3):
                        s2_copy(it, side, d, chunk, chunk).start()
                else:
                    d = (chunk - (x if side == 0 else y) + SIDE) % SIDE

                    @pl.when(d != 0)
                    def _():
                        s2_copy(it, side, d, chunk, 0).start()

        small_start(it, 1, small_sum(it, 0))
        if it + 1 < ITERS:
            more_maps((2,) if it == 0 else (5,))

        def sum_of(side, chunk, slot):
            block = p2[it, side, chunk]
            for e in range(SIDE - 1):
                block = block + r2[it, side, e, slot]
            return block

        if it + 1 < ITERS:
            for chunk in range(SIDE):
                wait_for(r2.at[it, :, :, chunk], s2_recv.at[chunk])
                for side in (0, 1):
                    images[it, on_line(side, chunk), half(side)] = sum_of(side, chunk, chunk)
                    for d in (2, 1, 3):
                        gather_copy(it, side, d, chunk).start()
            wait_for(r2.at[it], s2_send.at[0])
        else:
            wait_for(r2.at[it, :, :, 0], s2_recv.at[0])
            image = jnp.concatenate([sum_of(0, x, 0), sum_of(1, y, 0)], axis=0)
            theta = jnp.sum(small_sum(it, 1)) / ENTRIES
            wave = waves[it, own] * scale
            wave = wave - step_size * (image - theta * wave)
            norm_out[...] = fold(wave * wave)
            for dx, dy in others:
                norm_copy(dx, dy).start()
            wait_for(r2.at[it, :, :, 0], s2_send.at[0])
        wait_for(r1.at[it], s1_send.at[0])

    energy = product(beside(wave.T), doubled(image))

    @pl.when(core == 0)
    def _():
        e_out[...] = energy
        core_copy(e_out, e_in, 1).start()

    @pl.when(core == 1)
    def _():
        core_copy(e_out, e_in, 1).wait_recv()
        n_out[...] = product(tt[...], doubled(product(beside(e_in[...]), tdup[...])))

    squares = norm_out[...]
    wait_for(norm_in, norm_recv.at[0])
    for slot in range(NS - 1):
        squares = squares + norm_in[slot]
    scale = scale_from(squares)
    energy_scale = scale / BK

    @pl.when(core == 0)
    def _():
        c_out[...] = jnp.full((8, BK), energy_scale, F32)
        core_copy(c_out, c_in, 2).start()

    out[0] = wave * scale

    @pl.when(core == 1)
    def _():
        core_copy(c_out, c_in, 2).wait_recv()
        lower = n_out[...] * c_in[0:1, 0:1]
        f_out[...] = energy * energy_scale + lower
        for d in range(CHIPS - 1, 0, -1):
            @pl.when(z + d < CHIPS)
            def _():
                up_copy(f_out, f_in, f_send, f_recv, d).start()

        out[1] = lower
        n_out[...] = jnp.zeros((BK, BK), F32)
        for d in range(1, CHIPS):
            @pl.when(z >= d)
            def _():
                up_copy(f_out, f_in, f_send, f_recv, d).wait_recv()
                n_out[...] += product(wt[d - 1], doubled(product(beside(f_in[d - 1]), wdup[d - 1])))

        core_copy(n_out, n_in, 3).start()
        out[1] += product(tt[...], doubled(product(beside(n_out[...]), tdup[...])))
        for d in range(1, CHIPS):
            @pl.when(z + d < CHIPS)
            def _():
                up_copy(f_out, f_in, f_send, f_recv, d).wait_send()

            if d < CHIPS - 1:
                @pl.when((z >= 1) & (z + d < CHIPS))
                def _():
                    up_copy(pair_out, pair_in, pair_send, pair_recv, d).wait_send()

        core_copy(n_out, n_in, 3).wait_send()

    @pl.when(core == 0)
    def _():
        core_copy(t_out, t_in, 0).wait_send()
        core_copy(e_out, e_in, 1).wait_send()
        core_copy(c_out, c_in, 2).wait_send()
        core_copy(n_out, n_in, 3).wait_recv()
        out[1] = n_in[...]

    wait_for(norm_in, norm_send.at[0])
    small_end(ITERS - 1)


def shards(wave_in, env_left, env_right, sector_charge, term_charge, term_live, transfer):
    vmem = pl.BlockSpec(memory_space=pltpu.VMEM)
    hbm = pl.BlockSpec(memory_space=pl.ANY)
    dma = pltpu.SemaphoreType.DMA
    square = pltpu.VMEM((BK, BK), F32)
    tile = pltpu.VMEM((8, BK), F32)
    both = pl.pallas_call(
        kernel,
        out_shape=jax.ShapeDtypeStruct((2, BK, BK), F32),
        in_specs=[hbm, hbm, hbm, hbm, hbm, hbm, hbm],
        out_specs=vmem,
        scratch_shapes=[
            pltpu.SMEM((2, NS), jnp.int32),
            pltpu.SMEM((2, SLOTS), jnp.int32),
            pltpu.SMEM((SLOTS,), jnp.int32),
            pltpu.SMEM((NS,), jnp.int32),
            pltpu.SMEM((NS,), jnp.int32),
            pltpu.SMEM((SLOTS * NS,), jnp.int32),
            pltpu.SMEM((SLOTS * NS,), jnp.int32),
            pltpu.SMEM((SLOTS * NS,), F32),
            pltpu.VMEM((SLOTS, NS, BK, BK), F32),
            pltpu.VMEM((SLOTS, NS, BK, BK), F32),
            square,
            pltpu.VMEM((SLOTS, NS, BK, 2 * BK), BF16),
            pltpu.VMEM((NS, 2 * BK, SLOTS * BK), BF16),
            pltpu.VMEM((SLOTS, NS, 2 * BK, BK), BF16),
            pltpu.VMEM((ITERS, NS, BK, BK), F32),
            pltpu.VMEM((ITERS, NS, BK, BK), F32),
            pltpu.VMEM((ITERS - 1, NS, BK, BK), F32),
            pltpu.VMEM((ITERS, 2, SIDE - 1, SIDE, HALF, BK), F32),
            pltpu.VMEM((ITERS, 2, SIDE, HALF, BK), F32),
            pltpu.VMEM((ITERS, 2, SIDE - 1, SIDE, HALF, BK), F32),
            pltpu.VMEM((ITERS, 2, 8, BK), F32),
            pltpu.VMEM((ITERS, 2, SIDE - 1, 8, BK), F32),
            tile,
            pltpu.VMEM((NS - 1, 8, BK), F32),
            square,
            square,
            square,
            pltpu.VMEM((CHIPS - 2, BK, BK), F32),
            pltpu.VMEM((2 * BK, 2 * BK), BF16),
            pltpu.VMEM((BK, 2 * BK), BF16),
            pltpu.VMEM((CHIPS - 1, 2 * BK, 2 * BK), BF16),
            pltpu.VMEM((CHIPS - 1, BK, 2 * BK), BF16),
            square,
            square,
            tile,
            tile,
            square,
            pltpu.VMEM((CHIPS - 1, BK, BK), F32),
            square,
            square,
            dma((5 + 2 * SLOTS,)),
            dma((1,)),
            dma((SIDE,)),
            dma((1,)),
            dma((SIDE,)),
            dma((1,)),
            dma((SIDE,)),
            dma((2,)),
            dma((2,)),
            dma((1,)),
            dma((1,)),
            dma((4,)),
            dma((4,)),
            dma((CHIPS - 2,)),
            dma((CHIPS - 2,)),
            dma((CHIPS - 1,)),
            dma((CHIPS - 1,)),
        ],
        compiler_params=pltpu.CompilerParams(
            collective_id=0, has_side_effects=True, vmem_limit_bytes=56 * 1024 * 1024
        ),
    )(sector_charge.T, term_charge.T, term_live, wave_in, env_left, env_right, transfer)
    block = (1, 1, BK, BK)
    return both[0].reshape(block), both[1].reshape(block)


def solution(mesh):
    in_specs = (
        P("seg", None, None, None),
        P("seg", "term", None, None, None),
        P("seg", "term", None, None, None),
        P(),
        P("term", None),
        P("term"),
        P("seg", None, None, None),
    )
    out_specs = (P("seg", "term", None, None), P("seg", "term", None, None))
    return jax.shard_map(shards, mesh=mesh, in_specs=in_specs, out_specs=out_specs, check_vma=False)
```

time: 89 us -> 82.1 us (0.922)
  Pallas kernels: 86.7 us -> 79.8 us
    pallas_call x1, Pallas kernels: 86.7 us -> 79.8 us  [shards(): pl.pallas_call(kernel, out_shape=jax.ShapeDtypeStruct((2, BK, BK), F32),...]
where the time goes in v3:
time: 82.1 us; the launch traced here: 81.9 us
  Pallas kernels  79.8 us (97%)
  local copies, waits for them, and re-layouts  1.53 us (2%)
    pallas_call x1, Pallas kernels, shards(): pl.pallas_call(kernel, out_shape=jax.ShapeDtypeStruct((2, BK, BK), F32),...  79.8 us

profile of v3, /device:TPU:1, one launch (start us, length us, event | category | flops | bytes accessed | tf_op | source)
XLA Modules:
  0.0 81.9 jit_solution(2219897723467374853)
XLA Ops:
  0.6 79.8 %shard_map.86 = f32[2,128,128]{2,1,0:T(8,128)} custom-call(s32[2,16]{1,0:T(2,128)} %bitcast.6, s32[2,4]{1,0:T(2,128)} %bitcast.7, s32[4]{0:T(128)} %live_hbm.1, f32[1,16,128,128]{3,2,1,0:T(8,128)} %wave_hbm.1, f32[1,4,16,128,128]{4,3,2,1,0:T(8,128)} %left_hbm.1, f32[1,4,16,128,128]{4,3,2,1,0:T(8,128)} %right_hbm.1, f32[1,16,128,128]{3,2,1,0:T(8,128)} %transfer_hbm.1), custom_call_target="tpu_custom_call" | custom-call | tf_op jit(solution)/shard_map/pallas_call | solution.py:456
  80.4 1.5 %slice_bitcast_fusion = (f32[1,1,128,128]{3,2,1,0:T(8,128)}, f32[1,1,128,128]{3,2,1,0:T(8,128)}) fusion(f32[2,128,128]{2,1,0:T(8,128)} %shard_map.86), kind=kLoop, calls=%fused_computation | loop fusion | bytes 262144 | tf_op jit(solution)/shard_map/reshape;squeeze | solution.py:525

commit v4 on v3

--- a/solution.py
+++ b/solution.py
@@ -15,6 +15,7 @@
 NS = 16
 SLOTS = 4
 NSEG = 16
+EARLY = 8
 CHIPS = NSEG // 2
 ENTRIES = float(NS * BK * BK)
 mean_eps = 1e-06
@@ -63,9 +64,9 @@
     sector_ref, term_ref, live_ref, code, place, source, target, mask,
     stage_l, stage_r, stage_t, lcat, rcat, inner, waves, image_parts, images,
     r1, p2, r2, small, small_in, norm_out, norm_in,
-    t_out, t_in, pair_out, pair_in, tdup, tt, wdup, wt, e_out, e_in, c_out, c_in, f_out, f_in, n_out, n_in,
+    t_out, t_in, pair_out, pair_in, tdup, tt, wdup, wt, e_out, e_in, lower_in, f_out, f_in, n_out, n_in,
     load_sem, s1_send, s1_recv, s2_send, s2_recv, g_send, g_recv,
-    small_send, small_recv, norm_send, norm_recv, core_send, core_recv, pair_send, pair_recv, f_send, f_recv,
+    small_send, small_recv, norm_send, norm_recv, lower_send, lower_recv, ready, core_send, core_recv, pair_send, pair_recv, f_send, f_recv,
 ):
     seg = lax.axis_index("seg")
     own = lax.axis_index("term")
@@ -75,7 +76,10 @@
     def at(dx, dy):
         return (seg, ((x + dx) % SIDE) * SIDE + (y + dy) % SIDE)
 
-    other_core = (seg + 1 - 2 * core, own)
+    def beyond(dx, dy):
+        return (seg + 1 - 2 * core, at(dx, dy)[1])
+
+    other_core = beyond(0, 0)
 
     load_w = pltpu.make_async_copy(wave_hbm.at[0], waves.at[0], load_sem.at[0])
     load_t = pltpu.make_async_copy(transfer_hbm.at[0, own], stage_t, load_sem.at[1])
@@ -96,48 +100,42 @@
     others = [(dx, dy) for dx in (2, 1, 3, 0) for dy in (2, 1, 3, 0) if (dx, dy) != (0, 0)]
     for dx, dy in others:
         pl.semaphore_signal(barrier, inc=1, device_id=at(dx, dy), device_id_type=MESH)
+    pl.semaphore_signal(barrier, inc=1, device_id=other_core, device_id_type=MESH)
+
+    @pl.when(core == 1)
+    def _():
+        for dx, dy in others:
+            pl.semaphore_signal(barrier, inc=1, device_id=beyond(dx, dy), device_id_type=MESH)
+
     for d in range(1, CHIPS):
-        pl.semaphore_signal(barrier, inc=1, device_id=((seg + 2 * d) % NSEG, own), device_id_type=MESH)
-    pl.semaphore_signal(barrier, inc=1, device_id=other_core, device_id_type=MESH)
-    greeted = len(others) + CHIPS
+        @pl.when(z + d < CHIPS)
+        def _():
+            pl.semaphore_signal(barrier, inc=1, device_id=((seg + 2 * d) % NSEG, own), device_id_type=MESH)
 
     for load in load_i:
         load.wait()
     for s in range(NS):
         code[s] = sector_ref[0, s] * CHARGES + sector_ref[1, s]
 
-    def find(c, carry):
+    def sector_at(up, down):
+        inside = (up >= 0) & (up < CHARGES) & (down >= 0) & (down < CHARGES)
+        return inside, place[jnp.where(inside, up * CHARGES + down, 0)]
+
+    def look_up(w, s):
+        up, down = sector_ref[0, s], sector_ref[1, s]
+        up_change, down_change = term_ref[0, w], term_ref[1, w]
+        inside, found = sector_at(up - up_change, down - down_change)
+        source[w * NS + s] = found
+        mask[w * NS + s] = jnp.where(inside, live_ref[w].astype(F32), jnp.float32(0))
+        target[w * NS + s] = sector_at(up + up_change, down + down_change)[1]
+
+    load_w.wait()
+
+    def add_square(t, total):
         found = jnp.int32(0)
         for s in range(NS):
-            found = jnp.where(code[s] == c, jnp.int32(s), found)
-        place[c] = found
-        return carry
-
-    lax.fori_loop(0, NS, find, 0)
-
-    def look_up(w, carry):
-        up_change, down_change = term_ref[0, w], term_ref[1, w]
-        alive = live_ref[w].astype(F32)
-
-        def one(s, carry):
-            def sector_at(up, down):
-                inside = (up >= 0) & (up < CHARGES) & (down >= 0) & (down < CHARGES)
-                return inside, place[jnp.where(inside, up * CHARGES + down, 0)]
-
-            up, down = sector_ref[0, s], sector_ref[1, s]
-            inside, found = sector_at(up - up_change, down - down_change)
-            source[w * NS + s] = found
-            mask[w * NS + s] = jnp.where(inside, alive, jnp.float32(0))
-            target[w * NS + s] = sector_at(up + up_change, down + down_change)[1]
-            return carry
-
-        return lax.fori_loop(0, NS, one, carry)
-
-    lax.fori_loop(0, SLOTS, look_up, 0)
-
-    load_w.wait()
-
-    def add_square(t, total):
+            found = jnp.where(code[s] == t, jnp.int32(s), found)
+        place[t] = found
         v = waves[0, t]
         return total + fold(v * v)
 
@@ -153,6 +151,7 @@
 
         def set_left(s, carry):
             lcat[w, s] = beside(stage_l[w, s])
+            look_up(w, s)
             return carry
 
         lax.fori_loop(0, NS, set_left, 0, unroll=2)
@@ -168,16 +167,6 @@
             src_ref=src, dst_ref=dst.at[d - 1], send_sem=send.at[d - 1], recv_sem=recv.at[d - 1],
             device_id=((seg + 2 * d) % NSEG, own), device_id_type=MESH,
         )
-
-    load_t.wait()
-    rows = lax.broadcasted_iota(jnp.int32, (BK, BK), 0)
-    columns = lax.broadcasted_iota(jnp.int32, (BK, BK), 1)
-    t_out[...] = stage_t[...] + jnp.where(rows == columns, jnp.float32(1), jnp.float32(0))
-    pl.semaphore_wait(barrier, greeted)
-
-    @pl.when(core == 0)
-    def _():
-        core_copy(t_out, t_in, 0).start()
 
     def set_map(d, value):
         wdup[d - 1] = doubled(value)
@@ -189,6 +178,10 @@
             own_map = t_out[...]
             tdup[...] = doubled(own_map)
             tt[...] = beside(own_map.T)
+            @pl.when(z < CHIPS - 1)
+            def _():
+                pl.semaphore_wait(ready, CHIPS - 1 - z)
+
             core_copy(t_out, t_in, 0).wait_recv()
             lower_map = t_in[...]
             set_map(1, lower_map)
@@ -265,6 +258,12 @@
             device_id=at(dx, dy), device_id_type=MESH,
         )
 
+    def lower_copy(dx, dy):
+        return pltpu.make_async_remote_copy(
+            src_ref=norm_out, dst_ref=lower_in.at[dx * SIDE + dy], send_sem=lower_send.at[0], recv_sem=lower_recv.at[0],
+            device_id=beyond(dx, dy), device_id_type=MESH,
+        )
+
     def left_half(t, v):
         left = jnp.concatenate([lcat[w, target[w * NS + t]] for w in range(SLOTS)], axis=0)
         high, low = split(product(left, doubled(v)))
@@ -279,24 +278,52 @@
 
     for it in range(ITERS):
         if it == 0:
-            def begin(t, carry):
+            def begin(t):
                 v = waves[0, t] * scale
                 waves[0, t] = v
                 left_half(t, v)
-                return carry
-
-            lax.fori_loop(0, NS, begin, 0, unroll=4)
-            scale = jnp.float32(1)
-            for w in range(SLOTS):
-                load_r[w].wait()
-
-                def set_right(s, carry):
+
+            def set_right(s):
+                for w in range(SLOTS):
                     high, low = split(stage_r[w, s] * mask[w * NS + s])
                     rcat[s, 0:BK, w * BK:(w + 1) * BK] = high
                     rcat[s, BK:2 * BK, w * BK:(w + 1) * BK] = low
-                    return carry
-
-                lax.fori_loop(0, NS, set_right, 0, unroll=2)
+
+            def begin_early(p, carry):
+                begin(2 * p)
+                begin(2 * p + 1)
+                return carry
+
+            def begin_late(p, carry):
+                begin(EARLY + p)
+                for j in range(NS // (NS - EARLY)):
+                    set_right(NS // (NS - EARLY) * p + j)
+                return carry
+
+            lax.fori_loop(0, EARLY // 2, begin_early, 0)
+            for load in load_r:
+                load.wait()
+            lax.fori_loop(0, NS - EARLY, begin_late, 0, unroll=2)
+            scale = jnp.float32(1)
+
+            load_t.wait()
+            rows = lax.broadcasted_iota(jnp.int32, (BK, BK), 0)
+            columns = lax.broadcasted_iota(jnp.int32, (BK, BK), 1)
+            t_out[...] = stage_t[...] + jnp.where(rows == columns, jnp.float32(1), jnp.float32(0))
+            pl.semaphore_wait(barrier, len(others) + 1 + z + (1 - core) * len(others))
+
+            @pl.when(core == 0)
+            def _():
+                core_copy(t_out, t_in, 0).start()
+
+            @pl.when(core == 1)
+            def _():
+                for d in range(1, CHIPS):
+                    @pl.when(z >= d)
+                    def _():
+                        pl.semaphore_signal(
+                            ready, inc=1, device_id=((seg - 2 * d + NSEG) % NSEG, own), device_id_type=MESH
+                        )
         else:
             theta = jnp.sum(small_sum(it - 1, 1)) / ENTRIES
 
@@ -374,6 +401,12 @@
             norm_out[...] = fold(wave * wave)
             for dx, dy in others:
                 norm_copy(dx, dy).start()
+
+            @pl.when(core == 0)
+            def _():
+                for dx, dy in others + [(0, 0)]:
+                    lower_copy(dx, dy).start()
+
             wait_for(r2.at[it, :, :, 0], s2_send.at[0])
         wait_for(r1.at[it], s1_send.at[0])
 
@@ -396,17 +429,15 @@
     scale = scale_from(squares)
     energy_scale = scale / BK
 
-    @pl.when(core == 0)
-    def _():
-        c_out[...] = jnp.full((8, BK), energy_scale, F32)
-        core_copy(c_out, c_in, 2).start()
-
     out[0] = wave * scale
 
     @pl.when(core == 1)
     def _():
-        core_copy(c_out, c_in, 2).wait_recv()
-        lower = n_out[...] * c_in[0:1, 0:1]
+        wait_for(lower_in, lower_recv.at[0])
+        lower_squares = lower_in[0]
+        for slot in range(1, NS):
+            lower_squares = lower_squares + lower_in[slot]
+        lower = n_out[...] * (scale_from(lower_squares) / BK)
         f_out[...] = energy * energy_scale + lower
         for d in range(CHIPS - 1, 0, -1):
             @pl.when(z + d < CHIPS)
@@ -421,7 +452,7 @@
                 up_copy(f_out, f_in, f_send, f_recv, d).wait_recv()
                 n_out[...] += product(wt[d - 1], doubled(product(beside(f_in[d - 1]), wdup[d - 1])))
 
-        core_copy(n_out, n_in, 3).start()
+        core_copy(n_out, n_in, 2).start()
         out[1] += product(tt[...], doubled(product(beside(n_out[...]), tdup[...])))
         for d in range(1, CHIPS):
             @pl.when(z + d < CHIPS)
@@ -433,14 +464,14 @@
                 def _():
                     up_copy(pair_out, pair_in, pair_send, pair_recv, d).wait_send()
 
-        core_copy(n_out, n_in, 3).wait_send()
+        core_copy(n_out, n_in, 2).wait_send()
 
     @pl.when(core == 0)
     def _():
         core_copy(t_out, t_in, 0).wait_send()
         core_copy(e_out, e_in, 1).wait_send()
-        core_copy(c_out, c_in, 2).wait_send()
-        core_copy(n_out, n_in, 3).wait_recv()
+        wait_for(lower_in, lower_send.at[0])
+        core_copy(n_out, n_in, 2).wait_recv()
         out[1] = n_in[...]
 
     wait_for(norm_in, norm_send.at[0])
@@ -493,8 +524,7 @@
             pltpu.VMEM((CHIPS - 1, BK, 2 * BK), BF16),
             square,
             square,
-            tile,
-            tile,
+            pltpu.VMEM((NS, 8, BK), F32),
             square,
             pltpu.VMEM((CHIPS - 1, BK, BK), F32),
             square,
@@ -510,8 +540,11 @@
             dma((2,)),
             dma((1,)),
             dma((1,)),
-            dma((4,)),
-            dma((4,)),
+            dma((1,)),
+            dma((1,)),
+            pltpu.SemaphoreType.REGULAR,
+            dma((3,)),
+            dma((3,)),
             dma((CHIPS - 2,)),
             dma((CHIPS - 2,)),
             dma((CHIPS - 1,)),

time: 82.1 us -> 79.9 us (0.973)
  Pallas kernels: 79.8 us -> 77.4 us
    pallas_call x1, Pallas kernels: 79.8 us -> 77.4 us  [shards(): pl.pallas_call(kernel, out_shape=jax.ShapeDtypeStruct((2, BK, BK), F32),...]
where the time goes in v4:
time: 79.9 us; the launch traced here: 79.6 us
  Pallas kernels  77.4 us (97%)
  local copies, waits for them, and re-layouts  1.53 us (2%)
    pallas_call x1, Pallas kernels, shards(): pl.pallas_call(kernel, out_shape=jax.ShapeDtypeStruct((2, BK, BK), F32),...  77.4 us

profile of v4, /device:TPU:1, one launch (start us, length us, event | category | flops | bytes accessed | tf_op | source)
XLA Modules:
  0.0 79.6 jit_solution(1844510411773718975)
XLA Ops:
  0.6 77.4 %shard_map.86 = f32[2,128,128]{2,1,0:T(8,128)} custom-call(s32[2,16]{1,0:T(2,128)} %bitcast.6, s32[2,4]{1,0:T(2,128)} %bitcast.7, s32[4]{0:T(128)} %live_hbm.1, f32[1,16,128,128]{3,2,1,0:T(8,128)} %wave_hbm.1, f32[1,4,16,128,128]{4,3,2,1,0:T(8,128)} %left_hbm.1, f32[1,4,16,128,128]{4,3,2,1,0:T(8,128)} %right_hbm.1, f32[1,16,128,128]{3,2,1,0:T(8,128)} %transfer_hbm.1), custom_call_target="tpu_custom_call" | custom-call | tf_op jit(solution)/shard_map/pallas_call | solution.py:487
  78.1 1.5 %slice_bitcast_fusion = (f32[1,1,128,128]{3,2,1,0:T(8,128)}, f32[1,1,128,128]{3,2,1,0:T(8,128)}) fusion(f32[2,128,128]{2,1,0:T(8,128)} %shard_map.86), kind=kLoop, calls=%fused_computation | loop fusion | bytes 262144 | tf_op jit(solution)/shard_map/reshape;squeeze | solution.py:558

commit v5 on v4

--- a/solution.py
+++ b/solution.py
@@ -364,19 +364,18 @@
                 for e in range(SIDE - 1):
                     block = block + r1[it, side, e, chunk]
                 p2[it, side, chunk] = block
-                if it + 1 < ITERS:
-                    for d in (2, 1, 3):
-                        s2_copy(it, side, d, chunk, chunk).start()
-                else:
+                if it + 1 == ITERS:
                     d = (chunk - (x if side == 0 else y) + SIDE) % SIDE
 
                     @pl.when(d != 0)
                     def _():
                         s2_copy(it, side, d, chunk, 0).start()
 
-        small_start(it, 1, small_sum(it, 0))
-        if it + 1 < ITERS:
-            more_maps((2,) if it == 0 else (5,))
+            if it + 1 < ITERS:
+                for d in (2, 1, 3):
+                    for side in (0, 1):
+                        s2_copy(it, side, d, chunk, chunk).start()
+
 
         def sum_of(side, chunk, slot):
             block = p2[it, side, chunk]
@@ -385,14 +384,18 @@
             return block
 
         if it + 1 < ITERS:
+            small_start(it, 1, small_sum(it, 0))
             for chunk in range(SIDE):
                 wait_for(r2.at[it, :, :, chunk], s2_recv.at[chunk])
                 for side in (0, 1):
                     images[it, on_line(side, chunk), half(side)] = sum_of(side, chunk, chunk)
-                    for d in (2, 1, 3):
+                for d in (2, 1, 3):
+                    for side in (0, 1):
                         gather_copy(it, side, d, chunk).start()
             wait_for(r2.at[it], s2_send.at[0])
+            more_maps((2,) if it == 0 else (5,))
         else:
+            small_start(it, 1, small_sum(it, 0))
             wait_for(r2.at[it, :, :, 0], s2_recv.at[0])
             image = jnp.concatenate([sum_of(0, x, 0), sum_of(1, y, 0)], axis=0)
             theta = jnp.sum(small_sum(it, 1)) / ENTRIES
@@ -446,7 +449,7 @@
 
         out[1] = lower
         n_out[...] = jnp.zeros((BK, BK), F32)
-        for d in range(1, CHIPS):
+        for d in range(CHIPS - 1, 0, -1):
             @pl.when(z >= d)
             def _():
                 up_copy(f_out, f_in, f_send, f_recv, d).wait_recv()

time: 79.9 us -> 80 us (level)
  no operation moved by 1% of the time
where the time goes in v5:
time: 80 us; the launch traced here: 79.6 us
  Pallas kernels  77.4 us (97%)
  local copies, waits for them, and re-layouts  1.53 us (2%)
    pallas_call x1, Pallas kernels, shards(): pl.pallas_call(kernel, out_shape=jax.ShapeDtypeStruct((2, BK, BK), F32),...  77.4 us

profile of v5, /device:TPU:1, one launch (start us, length us, event | category | flops | bytes accessed | tf_op | source)
XLA Modules:
  0.0 79.6 jit_solution(2641062604203023683)
XLA Ops:
  0.6 77.4 %shard_map.86 = f32[2,128,128]{2,1,0:T(8,128)} custom-call(s32[2,16]{1,0:T(2,128)} %bitcast.6, s32[2,4]{1,0:T(2,128)} %bitcast.7, s32[4]{0:T(128)} %live_hbm.1, f32[1,16,128,128]{3,2,1,0:T(8,128)} %wave_hbm.1, f32[1,4,16,128,128]{4,3,2,1,0:T(8,128)} %left_hbm.1, f32[1,4,16,128,128]{4,3,2,1,0:T(8,128)} %right_hbm.1, f32[1,16,128,128]{3,2,1,0:T(8,128)} %transfer_hbm.1), custom_call_target="tpu_custom_call" | custom-call | tf_op jit(solution)/shard_map/pallas_call | solution.py:490
  78.1 1.5 %slice_bitcast_fusion = (f32[1,1,128,128]{3,2,1,0:T(8,128)}, f32[1,1,128,128]{3,2,1,0:T(8,128)}) fusion(f32[2,128,128]{2,1,0:T(8,128)} %shard_map.86), kind=kLoop, calls=%fused_computation | loop fusion | bytes 262144 | tf_op jit(solution)/shard_map/reshape;squeeze | solution.py:561

commit v6 on v5

--- a/solution.py
+++ b/solution.py
@@ -84,17 +84,17 @@
     load_w = pltpu.make_async_copy(wave_hbm.at[0], waves.at[0], load_sem.at[0])
     load_t = pltpu.make_async_copy(transfer_hbm.at[0, own], stage_t, load_sem.at[1])
     load_i = [
-        pltpu.make_async_copy(sector_hbm, sector_ref, load_sem.at[10]),
-        pltpu.make_async_copy(term_hbm, term_ref, load_sem.at[11]),
-        pltpu.make_async_copy(live_hbm, live_ref, load_sem.at[12]),
+        pltpu.make_async_copy(sector_hbm, sector_ref, load_sem.at[7]),
+        pltpu.make_async_copy(term_hbm, term_ref, load_sem.at[8]),
+        pltpu.make_async_copy(live_hbm, live_ref, load_sem.at[9]),
     ]
     for load in load_i:
         load.start()
     load_w.start()
     load_t.start()
     load_l = [pltpu.make_async_copy(left_hbm.at[0, w], stage_l.at[w], load_sem.at[2 + w]) for w in range(SLOTS)]
-    load_r = [pltpu.make_async_copy(right_hbm.at[0, w], stage_r.at[w], load_sem.at[6 + w]) for w in range(SLOTS)]
-    for load in load_l + load_r:
+    load_r = pltpu.make_async_copy(right_hbm.at[0], stage_r, load_sem.at[6])
+    for load in load_l + [load_r]:
         load.start()
     barrier = pltpu.get_barrier_semaphore()
     others = [(dx, dy) for dx in (2, 1, 3, 0) for dy in (2, 1, 3, 0) if (dx, dy) != (0, 0)]
@@ -301,8 +301,7 @@
                 return carry
 
             lax.fori_loop(0, EARLY // 2, begin_early, 0)
-            for load in load_r:
-                load.wait()
+            load_r.wait()
             lax.fori_loop(0, NS - EARLY, begin_late, 0, unroll=2)
             scale = jnp.float32(1)
 
@@ -410,8 +409,8 @@
                 for dx, dy in others + [(0, 0)]:
                     lower_copy(dx, dy).start()
 
-            wait_for(r2.at[it, :, :, 0], s2_send.at[0])
-        wait_for(r1.at[it], s1_send.at[0])
+        if it + 1 < ITERS:
+            wait_for(r1.at[it], s1_send.at[0])
 
     energy = product(beside(wave.T), doubled(image))
 
@@ -442,14 +441,14 @@
             lower_squares = lower_squares + lower_in[slot]
         lower = n_out[...] * (scale_from(lower_squares) / BK)
         f_out[...] = energy * energy_scale + lower
-        for d in range(CHIPS - 1, 0, -1):
+        for d in (4, 5, 3, 6, 2, 7, 1):
             @pl.when(z + d < CHIPS)
             def _():
                 up_copy(f_out, f_in, f_send, f_recv, d).start()
 
         out[1] = lower
         n_out[...] = jnp.zeros((BK, BK), F32)
-        for d in range(CHIPS - 1, 0, -1):
+        for d in (4, 5, 3, 6, 2, 7, 1):
             @pl.when(z >= d)
             def _():
                 up_copy(f_out, f_in, f_send, f_recv, d).wait_recv()
@@ -478,6 +477,8 @@
         out[1] = n_in[...]
 
     wait_for(norm_in, norm_send.at[0])
+    wait_for(r2.at[ITERS - 1, :, :, 0], s2_send.at[0])
+    wait_for(r1.at[ITERS - 1], s1_send.at[0])
     small_end(ITERS - 1)
 
 
@@ -532,7 +533,7 @@
             pltpu.VMEM((CHIPS - 1, BK, BK), F32),
             square,
             square,
-            dma((5 + 2 * SLOTS,)),
+            dma((6 + SLOTS,)),
             dma((1,)),
             dma((SIDE,)),
             dma((1,)),

time: 80 us -> 79.7 us (level)
  no operation moved by 1% of the time
where the time goes in v6:
time: 79.7 us; the launch traced here: 79.6 us
  Pallas kernels  77.4 us (97%)
  local copies, waits for them, and re-layouts  1.53 us (2%)
    pallas_call x1, Pallas kernels, shards(): pl.pallas_call(kernel, out_shape=jax.ShapeDtypeStruct((2, BK, BK), F32),...  77.4 us

profile of v6, /device:TPU:1, one launch (start us, length us, event | category | flops | bytes accessed | tf_op | source)
XLA Modules:
  0.0 79.6 jit_solution(2616316435734793195)
XLA Ops:
  0.6 77.4 %shard_map.86 = f32[2,128,128]{2,1,0:T(8,128)} custom-call(s32[2,16]{1,0:T(2,128)} %bitcast.6, s32[2,4]{1,0:T(2,128)} %bitcast.7, s32[4]{0:T(128)} %live_hbm.1, f32[1,16,128,128]{3,2,1,0:T(8,128)} %wave_hbm.1, f32[1,4,16,128,128]{4,3,2,1,0:T(8,128)} %left_hbm.1, f32[1,4,16,128,128]{4,3,2,1,0:T(8,128)} %right_hbm.1, f32[1,16,128,128]{3,2,1,0:T(8,128)} %transfer_hbm.1), custom_call_target="tpu_custom_call" | custom-call | tf_op jit(solution)/shard_map/pallas_call | solution.py:491
  78.0 1.5 %slice_bitcast_fusion = (f32[1,1,128,128]{3,2,1,0:T(8,128)}, f32[1,1,128,128]{3,2,1,0:T(8,128)}) fusion(f32[2,128,128]{2,1,0:T(8,128)} %shard_map.86), kind=kLoop, calls=%fused_computation | loop fusion | bytes 262144 | tf_op jit(solution)/shard_map/reshape;squeeze | solution.py:562
